TPU v7x, 32 devices: a whole 2x2x4 slice. The times are simulated.
32 devices in a mesh: abl: 2 (over y), head: 4 (over x, core), ctx: 4 (over z).
Axes of the slice: x: 2, y: 2, z: 4, core: 2. Of those that a mesh axis runs over, the one named last changes fastest.
Arguments:
- queries: bfloat16 [1024, 6144], P(('abl', 'head', 'ctx')), parts along dimension 0, may hold values from -30 to 30
- keys: bfloat16 [16384, 6144], P(('abl', 'ctx'), 'head'), parts along dimension 0, may hold values from -6 to 6
- values: bfloat16 [16384, 6144], P(('abl', 'ctx'), 'head'), parts along dimension 0, may hold values from -6 to 6
- kept_rows: int32 [128], P(('abl', 'ctx')), parts along dimension 0, may hold values from 0 to 1, as said below
- out_weight: bfloat16 [6144, 6144], P('head'), may hold values from -6 to 6
Outputs:
- projected: bfloat16 [1024, 6144], P(('abl', 'head', 'ctx')), parts along dimension 0
There are 2 independent parts, one for each index of `abl`. A program takes and returns all parts, laid end to end along the dimension named above; an argument that names none is the same for every part. Nothing has to cross between parts.
Inputs may be any that keep to these rules, and one draw needn't show every extreme that they name: `kept_rows`: in every part the first row of each block of 16 consecutive rows is kept.
All inputs are finite; a program needn't handle non-finite values.
Results may differ from a plain program's by a relative error of at most 0.028.
Values may be sent and summed in bfloat16 or wider, within the bound.
A program may use at most 128 MiB of HBM per device.

v0:
```python
import math

import jax
import jax.numpy as jnp
from jax import lax
from jax.sharding import PartitionSpec as P

HD = 128


def shards(queries, keys, values, kept_rows, out_weight):
    score_scale = 1.0 / math.sqrt(HD)
    local_heads = keys.shape[1] // HD
    key_count = keys.shape[0]
    key_heads = keys.reshape(key_count, local_heads, HD)
    value_heads = values.reshape(key_count, local_heads, HD)
    visible = jnp.repeat(kept_rows, 128) > 0
    query_block = lax.all_to_all(queries, "head", split_axis=1, concat_axis=0, tiled=True)
    all_queries = lax.all_gather(query_block, "ctx", axis=0, tiled=True)
    row_count = all_queries.shape[0]
    zeros_sum = jnp.zeros((row_count, local_heads * HD), jnp.float32)
    lowest = jnp.full((local_heads, row_count), -1e30, jnp.float32)
    summed = zeros_sum
    row_count = all_queries.shape[0]
    shaped = all_queries.reshape(row_count, local_heads, HD)
    scores = (
        jnp.einsum("qhd,khd->hqk", shaped, key_heads, preferred_element_type=jnp.float32)
        * score_scale
    )
    scores = jnp.where(visible[None, None, :], scores, -jnp.inf)
    highest = jnp.maximum(lowest, jnp.max(scores, axis=-1))
    rescale = jnp.exp(lowest - highest)
    softened = jnp.exp(scores - highest[..., None])
    normal_sum = jnp.sum(softened, axis=-1)
    mixed = jnp.einsum(
        "hqk,khd->qhd",
        softened.astype(jnp.bfloat16),
        value_heads,
        preferred_element_type=jnp.float32,
    )
    summed = summed * jnp.repeat(rescale.T, HD, axis=1) + mixed.reshape(row_count, local_heads * HD)
    summed, running, normal_sum = (summed, highest, normal_sum)
    highest = lax.pmax(running, "ctx")
    rescale = jnp.exp(running - highest)
    summed = summed * jnp.repeat(rescale.T, HD, axis=1)
    normal_sum = normal_sum * rescale
    summed, normal_sum = (
        lax.psum_scatter(
            summed.astype(jnp.bfloat16), "ctx", scatter_dimension=0, tiled=True
        ).astype(jnp.float32),
        lax.psum_scatter(
            normal_sum.astype(jnp.bfloat16), "ctx", scatter_dimension=1, tiled=True
        ).astype(jnp.float32),
    )
    attended = (summed / jnp.repeat(normal_sum.T, HD, axis=1)).astype(jnp.bfloat16)
    return lax.psum_scatter(
        jnp.dot(attended, out_weight, preferred_element_type=jnp.float32).astype(jnp.bfloat16),
        "head",
        scatter_dimension=0,
        tiled=True,
    )


def solution(mesh):
    placed = (
        P(("abl", "head", "ctx"), None),
        P(("abl", "ctx"), "head"),
        P(("abl", "ctx"), "head"),
        P(("abl", "ctx")),
        P("head", None),
    )
    return jax.shard_map(
        shards,
        mesh=mesh,
        in_specs=placed,
        out_specs=P(("abl", "head", "ctx"), None),
        check_vma=False,
    )
```

profile of v0, /device:TPU:0, one launch (start us, length us, event | category | flops | bytes accessed | tf_op | source)
XLA Modules:
  0.0 223.1 jit_solution(14071060724346164999)
XLA Ops:
  6.5 0.0 copy-start
  6.5 0.0 all-gather.2.cloned.1.call-start
  6.5 1.0 copy.33
  7.6 11.6 %all_to_all.19 = bf16[32,4,1536]{2,0,1:T(8,128)(2,1)} all-to-all(bf16[32,4,1536]{2,0,1:T(8,128)(2,1)S(1)} %bitcast.42), channel_id=1, replica_groups=mesh['abl'=2,'head'=4,'ctx'=4] {'head'}, dimensions={1} | all-to-all | bytes 786432 | tf_op jit(solution)/shard_map/all_to_all | solution.py:18
  19.1 0.0 all-gather.2.cloned.1.call-update
  19.2 0.0 reduce-scatter.12.cloned.1.call-start
  19.2 8.8 %copy.21 = bf16[2048,1536]{0,1:T(8,128)(2,1)} copy(bf16[2048,1536]{1,0:T(8,128)(2,1)} %param.6) | data formatting | bytes 12582912 | tf_op args[1]
  28.0 8.8 %copy.24 = bf16[2048,1536]{0,1:T(8,128)(2,1)} copy(bf16[2048,1536]{1,0:T(8,128)(2,1)} %param.7) | data formatting | bytes 12582912 | tf_op args[2]
  36.7 0.0 copy-done
  36.7 0.1 broadcast_bitcast_fusion
  36.8 20.3 %all-gather.2.cloned.1.call-done = bf16[512,1536]{1,0:T(8,128)(2,1)} async-done(((bf16[128,1536]{1,0:T(8,128)(2,1)}), bf16[512,1536]{1,0:T(8,128)(2,1)}) %all-gather.2.cloned.1.call-update) | async-done | bytes 1572880 | tf_op jit(solution)/shard_map/all_gather | solution.py:19
  57.1 1.7 copy.20
  58.8 22.6 %fusion = (f32[12,512]{1,0:T(8,128)S(1)}, f32[12,512,2048]{2,1,0:T(8,128)}) fusion(pred[2048]{0:T(1024)(128)(4,1)S(1)} %broadcast_bitcast_fusion, bf16[512,12,128]{0,2,1:T(8,128)(2,1)S(1)} %bitcast.38, bf16[2048,12,128]{0,2,1:T(8,128)(2,1)} %bitcast.37), kind=kOutput, calls=%fused_computation.2 | convolution fusion | flops 3258968064 | bytes 58222592 | tf_op jit(solution)/shard_map/qhd,khd->hqk/dot_general | solution.py:27
  81.4 16.9 %pmax.7 = f32[12,512]{1,0:T(8,128)S(1)} all-reduce(f32[12,512]{1,0:T(8,128)S(1)} %broadcast_maximum_fusion), channel_id=1, replica_groups=mesh['abl'=2,'head'=4,'ctx'=4] {'ctx'}, use_global_device_ids=true, to_apply=%region_1.2 | all-reduce | flops 6144 | bytes 49152 | tf_op jit(solution)/shard_map/pmax | solution.py:43
  98.4 21.1 %fusion.1 = f32[12,512]{1,0:T(8,128)S(1)} fusion(f32[12,512,2048]{2,1,0:T(8,128)} %get-tuple-element.9, f32[12,512]{1,0:T(8,128)S(1)} %broadcast_maximum_fusion, pred[2048]{0:T(1024)(128)(4,1)S(1)} %broadcast_bitcast_fusion), kind=kLoop, calls=%fused_computation.3 | loop fusion | flops 50325504 | bytes 50382848 | tf_op jit(solution)/shard_map/reduce_sum | solution.py:34
  119.5 0.8 copy.29
  120.3 0.0 reduce-scatter.12.cloned.1.call-update
  120.3 0.0 reduce-scatter.10.cloned.1.call-start
  120.4 22.0 %fusion.7 = bf16[512,12,128]{0,2,1:T(8,128)(2,1)S(1)} fusion(bf16[2048,12,128]{0,2,1:T(8,128)(2,1)} %bitcast.39, f32[12,512,2048]{2,1,0:T(8,128)} %get-tuple-element.9, f32[12,512]{1,0:T(8,128)S(1)} %broadcast_maximum_fusion, pred[2048]{0:T(1024)(128)(4,1)S(1)} %broadcast_bitcast_fusion, f32[512,12]{0,1:T(8,128)S(1)} %get-tuple-element.6, ...), kind=kOutput, calls=%fused_computation.10 | convolution fusion | flops 3273916416 | bytes 58271744 | tf_op jit(solution)/shard_map/hqk,khd->qhd/dot_general | solution.py:35
  142.4 1.6 copy.27
  144.0 0.0 reduce-scatter.10.cloned.1.call-update
  144.0 0.2 reduce-scatter.8.cloned.1.call-start
  144.2 0.0 reduce-scatter.12.cloned.1.call-done
  144.3 0.8 copy.30
  145.1 32.7 %reduce-scatter.10.cloned.1.call-done = bf16[128,1536]{1,0:T(8,128)(2,1)} async-done(((bf16[512,1536]{1,0:T(8,128)(2,1)}), bf16[128,1536]{1,0:T(8,128)(2,1)}) %reduce-scatter.10.cloned.1.call-update) | async-done | bytes 393232
  177.7 1.2 copy.28
  179.0 0.1 fusion.10
  179.1 10.2 %convolution_convert_fusion = bf16[128,6144]{1,0:T(8,128)(2,1)} fusion(bf16[128,1536]{0,1:T(8,128)(2,1)S(1)} %fusion.10, bf16[1536,6144]{1,0:T(8,128)(2,1)} %param.9), kind=kOutput, calls=%fused_computation.7 | convolution fusion | flops 2416705536 | bytes 20840448 | tf_op jit(solution)/shard_map/dot_general | solution.py:57
  189.3 0.0 reduce-scatter.8.cloned.1.call-update
  189.3 27.3 %reduce-scatter.8.cloned.1.call-done = bf16[32,6144]{1,0:T(8,128)(2,1)} async-done(((bf16[128,6144]{1,0:T(8,128)(2,1)}), bf16[32,6144]{1,0:T(8,128)(2,1)}) %reduce-scatter.8.cloned.1.call-update) | async-done | bytes 393232 | tf_op jit(solution)/shard_map/reduce_scatter | solution.py:56
  (4 shorter events, 0.0 us)
Async XLA Ops:
  6.5 30.2 %copy-start = (s32[16]{0:T(128)S(1)}, s32[16]{0:T(128)}, u32[]{:S(2)}) copy-start(s32[16]{0:T(128)} %param.8) | copy-start | bytes 196
  6.5 50.6 %all-gather.2.cloned.1.call-start = ((), (), s32[]{:S(2)}) async-start(), calls=%async_computation.4 | async-start | bytes 1966080 | tf_op jit(solution)/shard_map/all_gather | solution.py:19
  19.2 125.1 %reduce-scatter.12.cloned.1.call-start = ((), (), s32[]{:S(2)}) async-start(), calls=%async_computation.7 | async-start | bytes 163840
  120.3 57.4 %reduce-scatter.10.cloned.1.call-start = ((), (), s32[]{:S(2)}) async-start(), calls=%async_computation.6 | async-start | bytes 1966080
  144.0 72.6 %reduce-scatter.8.cloned.1.call-start = ((), (), s32[]{:S(2)}) async-start(), calls=%async_computation.5 | async-start | bytes 1966080 | tf_op jit(solution)/shard_map/reduce_scatter | solution.py:56
Sparse Core Ops, SparseCore 0:
  19.3 37.8 all-gather.1
  120.4 17.4 reduce-scatter.11
  144.1 33.5 reduce-scatter.9
  189.4 27.1 reduce-scatter.7
where the time goes:
time: 224 us; the launch traced here: 223 us
  waiting for transfers between devices  80.4 us (36%)
  matrix products  54.9 us (25%)
  blocking collectives  28.5 us (13%)
  local copies, waits for them, and re-layouts  24.7 us (11%)
  other arithmetic  21.2 us (9%)
  between operations  13.2 us (6%)
    unnamed x6, waiting for transfers between devices  32.7 us
    reduce_scatter x1, waiting for transfers between devices, shards(): lax.psum_scatter(jnp.dot(attended, out_weight, preferred_element_type=jnp...  27.3 us
    dot_general x1, matrix products, shards(): jnp.einsum('qhd,khd->hqk', shaped, key_heads, preferred_element_type=jnp....  22.6 us
    dot_general x1, matrix products, shards(): jnp.einsum('hqk,khd->qhd', softened.astype(jnp.bfloat16), value_heads, pr...  22 us
    unnamed x8, local copies, waits for them, and re-layouts  21.9 us
    reduce_sum x1, other arithmetic, shards(): normal_sum = jnp.sum(softened, axis=-1)  21.1 us
    all_gather x1, waiting for transfers between devices, shards(): all_queries = lax.all_gather(query_block, 'ctx', axis=0, tiled=True)  20.3 us
    pmax x1, blocking collectives, shards(): highest = lax.pmax(running, 'ctx')  16.9 us
  transfers between devices with their start and end apart: 4, of which 3 were waited for; matrix products, arithmetic and copies ran while one was open for 19% of the time, Pallas kernels for 0%

commit v1 on v0

--- a/solution.py
+++ b/solution.py
@@ -1,14 +1,19 @@
+import functools
 import math
 
 import jax
 import jax.numpy as jnp
 from jax import lax
+from jax.experimental import pallas as pl
+from jax.experimental.pallas import tpu as pltpu
 from jax.sharding import PartitionSpec as P
 
 HD = 128
-
-
-def shards(queries, keys, values, kept_rows, out_weight):
+MESH = pl.DeviceIdType.MESH
+SCALE2 = math.log2(math.e) / math.sqrt(HD)
+
+
+def general_shards(queries, keys, values, kept_rows, out_weight):
     score_scale = 1.0 / math.sqrt(HD)
     local_heads = keys.shape[1] // HD
     key_count = keys.shape[0]
@@ -18,19 +23,14 @@
     query_block = lax.all_to_all(queries, "head", split_axis=1, concat_axis=0, tiled=True)
     all_queries = lax.all_gather(query_block, "ctx", axis=0, tiled=True)
     row_count = all_queries.shape[0]
-    zeros_sum = jnp.zeros((row_count, local_heads * HD), jnp.float32)
-    lowest = jnp.full((local_heads, row_count), -1e30, jnp.float32)
-    summed = zeros_sum
-    row_count = all_queries.shape[0]
     shaped = all_queries.reshape(row_count, local_heads, HD)
     scores = (
         jnp.einsum("qhd,khd->hqk", shaped, key_heads, preferred_element_type=jnp.float32)
         * score_scale
     )
     scores = jnp.where(visible[None, None, :], scores, -jnp.inf)
-    highest = jnp.maximum(lowest, jnp.max(scores, axis=-1))
-    rescale = jnp.exp(lowest - highest)
-    softened = jnp.exp(scores - highest[..., None])
+    running = jnp.max(scores, axis=-1)
+    softened = jnp.exp(scores - running[..., None])
     normal_sum = jnp.sum(softened, axis=-1)
     mixed = jnp.einsum(
         "hqk,khd->qhd",
@@ -38,8 +38,7 @@
         value_heads,
         preferred_element_type=jnp.float32,
     )
-    summed = summed * jnp.repeat(rescale.T, HD, axis=1) + mixed.reshape(row_count, local_heads * HD)
-    summed, running, normal_sum = (summed, highest, normal_sum)
+    summed = mixed.reshape(row_count, local_heads * HD)
     highest = lax.pmax(running, "ctx")
     rescale = jnp.exp(running - highest)
     summed = summed * jnp.repeat(rescale.T, HD, axis=1)
@@ -61,7 +60,257 @@
     )
 
 
+def kernel(
+    q_ref, k_hbm, v_hbm, kept_ref, w_hbm, out_ref,
+    kbuf, vbuf, wbuf, qbuf, abuf, sbuf, rbuf, srbuf, bias, att, pbuf, sib, xsend, xrecv,
+    kv_sem, w_sem, a2a_s, a2a_r, ag_s, ag_r, rs_s, rs_r, st_s, st_r, sib_s, sib_r, x_s, x_r,
+):
+    heads, ctxs = 4, qbuf.shape[1]
+    groups, _, block, cw = qbuf.shape
+    rows = q_ref.shape[0]
+    hg = groups * cw
+    per = cw // HD
+    ncols, _, _, nw = pbuf.shape
+    h = lax.axis_index("head")
+    c = lax.axis_index("ctx")
+
+    def kv_copies(g):
+        cols = pl.ds(pl.multiple_of(g * cw, cw), cw)
+        return (
+            pltpu.make_async_copy(k_hbm.at[:, cols], kbuf.at[g], kv_sem.at[0, g]),
+            pltpu.make_async_copy(v_hbm.at[:, cols], vbuf.at[g], kv_sem.at[1, g]),
+        )
+
+    def w_copy(n):
+        cols = pl.ds(pl.multiple_of(n * nw, nw), nw)
+        return pltpu.make_async_copy(w_hbm.at[:, cols], wbuf.at[n], w_sem.at[n])
+
+    def a2a(g, d, sender, target):
+        return pltpu.make_async_remote_copy(
+            src_ref=q_ref.at[:, pl.ds(pl.multiple_of(target * hg + g * cw, cw), cw)],
+            dst_ref=qbuf.at[g, c, pl.ds(pl.multiple_of(sender * rows, rows), rows), :],
+            send_sem=a2a_s.at[g, d - 1], recv_sem=a2a_r.at[g, d - 1],
+            device_id={"head": target}, device_id_type=MESH)
+
+    def gather(g, d, sender, target):
+        return pltpu.make_async_remote_copy(
+            src_ref=qbuf.at[g, sender], dst_ref=qbuf.at[g, sender],
+            send_sem=ag_s.at[g, d - 1], recv_sem=ag_r.at[g, d - 1],
+            device_id={"ctx": target}, device_id_type=MESH)
+
+    def scatter(g, d, target):
+        return (
+            pltpu.make_async_remote_copy(
+                src_ref=abuf.at[g, target], dst_ref=rbuf.at[g, d - 1],
+                send_sem=rs_s.at[g, d - 1], recv_sem=rs_r.at[g, d - 1],
+                device_id={"ctx": target}, device_id_type=MESH),
+            pltpu.make_async_remote_copy(
+                src_ref=sbuf.at[g, target], dst_ref=srbuf.at[g, d - 1],
+                send_sem=st_s.at[g, d - 1], recv_sem=st_r.at[g, d - 1],
+                device_id={"ctx": target}, device_id_type=MESH),
+        )
+
+    sibling = h + 1 - 2 * lax.rem(h, 2)
+    across = lax.rem(h + 2, 4)
+    diagonal = lax.rem(sibling + 2, 4)
+
+    def to_sibling(n, i):
+        return pltpu.make_async_remote_copy(
+            src_ref=pbuf.at[n, sibling if i else diagonal], dst_ref=sib.at[n, i],
+            send_sem=sib_s.at[n, i], recv_sem=sib_r.at[n, i],
+            device_id={"head": sibling}, device_id_type=MESH)
+
+    def to_across(n):
+        return pltpu.make_async_remote_copy(
+            src_ref=xsend.at[n], dst_ref=xrecv.at[n],
+            send_sem=x_s.at[n], recv_sem=x_r.at[n],
+            device_id={"head": across}, device_id_type=MESH)
+
+    barrier = pltpu.get_barrier_semaphore()
+    for d in range(1, heads):
+        pl.semaphore_signal(barrier, inc=1, device_id={"head": lax.rem(h + d, heads)}, device_id_type=MESH)
+    for d in range(1, ctxs):
+        pl.semaphore_signal(barrier, inc=1, device_id={"ctx": lax.rem(c + d, ctxs)}, device_id_type=MESH)
+
+    @pl.loop(0, groups)
+    def _(g):
+        for copy in kv_copies(g):
+            copy.start()
+
+    pl.semaphore_wait(barrier, heads + ctxs - 2)
+
+    @pl.loop(0, groups)
+    def _(g):
+        for d in (2, 1, 3):
+            a2a(g, d, h, lax.rem(h + d, heads)).start()
+        qbuf[g, c, pl.ds(pl.multiple_of(h * rows, rows), rows), :] = q_ref[
+            :, pl.ds(pl.multiple_of(h * hg + g * cw, cw), cw)]
+
+    @pl.loop(0, ncols)
+    def _(n):
+        w_copy(n).start()
+
+    for i in range(kept_ref.shape[0]):
+        bias[:, i * 128:(i + 1) * 128] = jnp.full(
+            (8, 128), jnp.where(kept_ref[i] > 0, 0.0, -jnp.inf), jnp.float32)
+
+    @pl.loop(0, groups)
+    def _(g):
+        for d in range(1, heads):
+            a2a(g, d, lax.rem(h + heads - d, heads), h).wait_recv()
+        for d in range(1, ctxs):
+            gather(g, d, c, lax.rem(c + d, ctxs)).start()
+
+    ones = jnp.ones((kbuf.shape[1], HD), jnp.bfloat16)
+    lane = lax.broadcasted_iota(jnp.int32, (2 * block, HD), 1)
+
+    @pl.loop(0, groups)
+    def _(g):
+        for d in range(1, ctxs):
+            gather(g, d, lax.rem(c + ctxs - d, ctxs), c).wait_recv()
+        for copy in kv_copies(g):
+            copy.wait()
+        stats = [jnp.zeros((2 * block, HD), jnp.float32) for _ in range(ctxs // 2)]
+        for j in range(per):
+            cols = slice(j * HD, (j + 1) * HD)
+            key_head = kbuf[g, :, cols]
+            value_head = jnp.concatenate([vbuf[g, :, cols], ones], axis=1)
+            for t in range(ctxs // 2):
+                query = qbuf[g, 2 * t:2 * t + 2, :, cols].reshape(2 * block, HD)
+                scores = lax.dot_general(
+                    query, key_head, (((1,), (1,)), ((), ())),
+                    preferred_element_type=jnp.float32) + bias[0:1, :]
+                highest = jnp.max(scores, axis=1, keepdims=True)
+                probs = jnp.exp2((scores - highest) * SCALE2)
+                mixed = jnp.dot(
+                    probs.astype(jnp.bfloat16), value_head, preferred_element_type=jnp.float32)
+                normal = mixed[:, HD:]
+                abuf[g, 2 * t:2 * t + 2, :, cols] = (
+                    (mixed[:, :HD] / normal).astype(jnp.bfloat16).reshape(2, block, HD))
+                stats[t] = jnp.where(lane == j, highest * SCALE2 + jnp.log2(normal), stats[t])
+        for t in range(ctxs // 2):
+            for u in range(2):
+                sbuf[g, 2 * t + u] = stats[t][u * block:(u + 1) * block].T[0:8, :]
+        for d in range(1, ctxs):
+            for copy in scatter(g, d, lax.rem(c + d, ctxs)):
+                copy.start()
+
+    @pl.loop(0, groups)
+    def _(g):
+        for d in range(1, ctxs):
+            for copy in scatter(g, d, lax.rem(c + d, ctxs)):
+                copy.wait_recv()
+        logs = jnp.concatenate(
+            [sbuf[g, c]] + [srbuf[g, d] for d in range(ctxs - 1)]
+            + [jnp.zeros((HD - 8 * ctxs, block), jnp.float32)], axis=0).T
+        parts = [abuf[g, c]] + [rbuf[g, d] for d in range(ctxs - 1)]
+        for j in range(per):
+            own = [logs[:, 8 * i + j:8 * i + j + 1] for i in range(ctxs)]
+            top = functools.reduce(jnp.maximum, own)
+            weights = [jnp.exp2(x - top) for x in own]
+            total = functools.reduce(jnp.add, weights)
+            value = functools.reduce(jnp.add, [
+                w * x[:, j * HD:(j + 1) * HD].astype(jnp.float32) for w, x in zip(weights, parts)])
+            att[g, :, j * HD:(j + 1) * HD] = (value / total).astype(jnp.bfloat16)
+
+    @pl.loop(0, ncols)
+    def _(n):
+        w_copy(n).wait()
+        total = functools.reduce(jnp.add, [
+            jnp.dot(att[g], wbuf[n, g * cw:(g + 1) * cw, :], preferred_element_type=jnp.float32)
+            for g in range(groups)])
+        pbuf[n] = total.astype(jnp.bfloat16).reshape(heads, rows, nw)
+        for i in range(2):
+            to_sibling(n, i).start()
+
+    @pl.loop(0, ncols)
+    def _(n):
+        to_sibling(n, 0).wait_recv()
+        xsend[n] = (pbuf[n, across].astype(jnp.float32) + sib[n, 0].astype(jnp.float32)).astype(jnp.bfloat16)
+        to_across(n).start()
+
+    for n in range(ncols):
+        to_sibling(n, 1).wait_recv()
+        to_across(n).wait_recv()
+        out_ref[:, n * nw:(n + 1) * nw] = (
+            pbuf[n, h].astype(jnp.float32) + sib[n, 1].astype(jnp.float32)
+            + xrecv[n].astype(jnp.float32)).astype(jnp.bfloat16)
+
+    @pl.loop(0, groups)
+    def _(g):
+        for d in range(1, heads):
+            a2a(g, d, h, lax.rem(h + d, heads)).wait_send()
+        for d in range(1, ctxs):
+            gather(g, d, c, lax.rem(c + d, ctxs)).wait_send()
+            for copy in scatter(g, d, lax.rem(c + d, ctxs)):
+                copy.wait_send()
+
+    @pl.loop(0, ncols)
+    def _(n):
+        to_sibling(n, 0).wait_send()
+        to_sibling(n, 1).wait_send()
+        to_across(n).wait_send()
+
+
+def fused_shards(ctxs, queries, keys, values, kept_rows, out_weight):
+    rows, width = queries.shape
+    key_count, hg = keys.shape
+    cw = 2 * HD
+    groups = hg // cw
+    block = 4 * rows
+    nw = 1024
+    ncols = width // nw
+    bf, f32 = jnp.bfloat16, jnp.float32
+    dma = pltpu.SemaphoreType.DMA
+    vmem = pl.BlockSpec(memory_space=pltpu.VMEM)
+    hbm = pl.BlockSpec(memory_space=pl.ANY)
+    return pl.pallas_call(
+        kernel,
+        out_shape=jax.ShapeDtypeStruct((rows, width), bf),
+        in_specs=[vmem, hbm, hbm, pl.BlockSpec(memory_space=pltpu.SMEM), hbm],
+        out_specs=vmem,
+        scratch_shapes=[
+            pltpu.VMEM((groups, key_count, cw), bf),
+            pltpu.VMEM((groups, key_count, cw), bf),
+            pltpu.VMEM((ncols, hg, nw), bf),
+            pltpu.VMEM((groups, ctxs, block, cw), bf),
+            pltpu.VMEM((groups, ctxs, block, cw), bf),
+            pltpu.VMEM((groups, ctxs, 8, block), f32),
+            pltpu.VMEM((groups, ctxs - 1, block, cw), bf),
+            pltpu.VMEM((groups, ctxs - 1, 8, block), f32),
+            pltpu.VMEM((8, key_count), f32),
+            pltpu.VMEM((groups, block, cw), bf),
+            pltpu.VMEM((ncols, 4, rows, nw), bf),
+            pltpu.VMEM((ncols, 2, rows, nw), bf),
+            pltpu.VMEM((ncols, rows, nw), bf),
+            pltpu.VMEM((ncols, rows, nw), bf),
+            dma((2, groups)), dma((ncols,)),
+            dma((groups, 3)), dma((groups, 3)),
+            dma((groups, ctxs - 1)), dma((groups, ctxs - 1)),
+            dma((groups, ctxs - 1)), dma((groups, ctxs - 1)),
+            dma((groups, ctxs - 1)), dma((groups, ctxs - 1)),
+            dma((ncols, 2)), dma((ncols, 2)),
+            dma((ncols,)), dma((ncols,)),
+        ],
+        compiler_params=pltpu.CompilerParams(
+            collective_id=0, has_side_effects=True, vmem_limit_bytes=60 * 2**20),
+        cost_estimate=pl.CostEstimate(
+            flops=4 * ctxs * block * key_count * hg + 2 * block * hg * width,
+            bytes_accessed=2 * (2 * key_count * hg + hg * width),
+            transcendentals=ctxs * block * key_count * hg // HD),
+        name="attention",
+    )(queries, keys, values, kept_rows, out_weight)
+
+
 def solution(mesh):
+    heads, ctxs = mesh.shape["head"], mesh.shape["ctx"]
+
+    def shards(queries, keys, values, kept_rows, out_weight):
+        rows = queries.shape[0]
+        if heads == 4 and ctxs == 4 and rows == 32 and keys.shape[1] % (2 * HD) == 0:
+            return fused_shards(ctxs, queries, keys, values, kept_rows, out_weight)
+        return general_shards(queries, keys, values, kept_rows, out_weight)
+
     placed = (
         P(("abl", "head", "ctx"), None),
         P(("abl", "ctx"), "head"),

time: 224 us -> 98 us (0.44)
  Pallas kernels: 0 us -> 96 us
  waiting for transfers between devices: 80.4 us -> 0 us
  matrix products: 54.9 us -> 0 us
  blocking collectives: 28.5 us -> 0 us
  local copies, waits for them, and re-layouts: 24.7 us -> 1.77 us
  other arithmetic: 21.2 us -> 0 us
  between operations: 13.2 us -> 0.01 us
    pallas_call x0 -> x1, Pallas kernels: none -> 96 us  [fused_shards(): pl.pallas_call(kernel, out_shape=jax.ShapeDtypeStruct((rows, width), bf),...]
    dot_general x3 -> x0, matrix products: 54.9 us -> none  [the longest x1 22.6 us: shards(): jnp.einsum('qhd,khd->hqk', shaped, key_heads, preferred_element_type=jnp....]
    unnamed x6 -> x0, waiting for transfers between devices: 32.7 us -> none
    reduce_scatter x1 -> x0, waiting for transfers between devices: 27.3 us -> none  [shards(): lax.psum_scatter(jnp.dot(attended, out_weight, preferred_element_type=jnp...]
    reduce_sum x1 -> x0, other arithmetic: 21.1 us -> none  [shards(): normal_sum = jnp.sum(softened, axis=-1)]
    all_gather x1 -> x0, waiting for transfers between devices: 20.3 us -> none  [shards(): all_queries = lax.all_gather(query_block, 'ctx', axis=0, tiled=True)]
    unnamed x8 -> x1, local copies, waits for them, and re-layouts: 21.9 us -> 1.77 us
    pmax x1 -> x0, blocking collectives: 16.9 us -> none  [shards(): highest = lax.pmax(running, 'ctx')]
  transfers between devices with their start and end apart: 4 -> 0, of which waited for: 3 -> 0; matrix products, arithmetic and copies ran while one was open for 19% -> 0% of each run, Pallas kernels for 0% -> 0%
where the time goes in v1:
time: 98 us; the launch traced here: 97.8 us
  Pallas kernels  96 us (98%)
  local copies, waits for them, and re-layouts  1.77 us (2%)
    pallas_call x1, Pallas kernels, fused_shards(): pl.pallas_call(kernel, out_shape=jax.ShapeDtypeStruct((rows, width), bf),...  96 us

profile of v1, /device:TPU:0, one launch (start us, length us, event | category | flops | bytes accessed | tf_op | source)
XLA Modules:
  0.0 97.8 jit_solution(6810034086715890378)
XLA Ops:
  0.0 96.0 %attention.1 = bf16[32,6144]{1,0:T(8,128)(2,1)} custom-call(bf16[32,6144]{1,0:T(8,128)(2,1)} %q_ref.1, bf16[2048,1536]{1,0:T(8,128)(2,1)} %k_hbm.1, bf16[2048,1536]{1,0:T(8,128)(2,1)} %v_hbm.1, s32[16]{0:T(128)} %kept_ref.1, bf16[1536,6144]{1,0:T(8,128)(2,1)} %w_hbm.1), custom_call_target="tpu_custom_call" | custom-call | flops 8858370048 | bytes 31457280 | tf_op jit(solution)/shard_map/attention/pallas_call | solution.py:267
  96.0 1.8 %copy.7 = bf16[32,6144]{1,0:T(8,128)(2,1)} copy(bf16[32,6144]{1,0:T(8,128)(2,1)} %attention.1) | data formatting | bytes 786432

commit v2 on v1

--- a/solution.py
+++ b/solution.py
@@ -61,13 +61,13 @@
 
 
 def kernel(
-    q_ref, k_hbm, v_hbm, kept_ref, w_hbm, out_ref,
+    q_hbm, k_hbm, v_hbm, kept_ref, w_hbm, out_ref,
     kbuf, vbuf, wbuf, qbuf, abuf, sbuf, rbuf, srbuf, bias, att, pbuf, sib, xsend, xrecv,
-    kv_sem, w_sem, a2a_s, a2a_r, ag_s, ag_r, rs_s, rs_r, st_s, st_r, sib_s, sib_r, x_s, x_r,
+    kv_sem, w_sem, own_sem, up_s, up_r, dn_s, dn_r, a2a_s, a2a_r, ag_s, ag_r, rs_s, rs_r, st_s, st_r, sib_s, sib_r, x_s, x_r,
 ):
     heads, ctxs = 4, qbuf.shape[1]
     groups, _, block, cw = qbuf.shape
-    rows = q_ref.shape[0]
+    rows = q_hbm.shape[0]
     hg = groups * cw
     per = cw // HD
     ncols, _, _, nw = pbuf.shape
@@ -87,16 +87,64 @@
 
     def a2a(g, d, sender, target):
         return pltpu.make_async_remote_copy(
-            src_ref=q_ref.at[:, pl.ds(pl.multiple_of(target * hg + g * cw, cw), cw)],
+            src_ref=q_hbm.at[:, pl.ds(pl.multiple_of(target * hg + g * cw, cw), cw)],
             dst_ref=qbuf.at[g, c, pl.ds(pl.multiple_of(sender * rows, rows), rows), :],
             send_sem=a2a_s.at[g, d - 1], recv_sem=a2a_r.at[g, d - 1],
             device_id={"head": target}, device_id_type=MESH)
 
-    def gather(g, d, sender, target):
-        return pltpu.make_async_remote_copy(
-            src_ref=qbuf.at[g, sender], dst_ref=qbuf.at[g, sender],
-            send_sem=ag_s.at[g, d - 1], recv_sem=ag_r.at[g, d - 1],
+    def own_copy(g):
+        return pltpu.make_async_copy(
+            q_hbm.at[:, pl.ds(pl.multiple_of(h * hg + g * cw, cw), cw)],
+            qbuf.at[g, c, pl.ds(pl.multiple_of(h * rows, rows), rows), :], own_sem.at[g])
+
+    def gather(d, sender, target):
+        return pltpu.make_async_remote_copy(
+            src_ref=qbuf.at[0, sender], dst_ref=qbuf.at[0, sender],
+            send_sem=ag_s.at[d - 1], recv_sem=ag_r.at[d - 1],
             device_id={"ctx": target}, device_id_type=MESH)
+
+    def up(g, k, part):
+        return pltpu.make_async_remote_copy(
+            src_ref=qbuf.at[g, part], dst_ref=qbuf.at[g, part],
+            send_sem=up_s.at[g, k], recv_sem=up_r.at[g, k],
+            device_id={"ctx": lax.rem(c + 1, ctxs)}, device_id_type=MESH)
+
+    def down(g, k, part):
+        return pltpu.make_async_remote_copy(
+            src_ref=qbuf.at[g, part], dst_ref=qbuf.at[g, part],
+            send_sem=dn_s.at[g, k], recv_sem=dn_r.at[g, k],
+            device_id={"ctx": lax.rem(c + ctxs - 1, ctxs)}, device_id_type=MESH)
+
+    last = ctxs - 1
+
+    def exchanged(g):
+        own_copy(g).wait()
+        for d in range(1, heads):
+            a2a(g, d, lax.rem(h + heads - d, heads), h).wait_recv()
+
+    def hop(g, k):
+        @pl.when(jnp.logical_and(c < last, c >= k))
+        def _():
+            if k:
+                up(g, k - 1, c - k).wait_recv()
+            up(g, k, c - k).start()
+
+        @pl.when(jnp.logical_and(c > 0, c + k <= last))
+        def _():
+            if k:
+                down(g, k - 1, c + k).wait_recv()
+            down(g, k, c + k).start()
+
+    def stage(s):
+        for k in range(last):
+            g = s - k
+            inside = jnp.logical_and(g >= 1, g < groups)
+
+            @pl.when(inside)
+            def _():
+                if k == 0:
+                    exchanged(g)
+                hop(g, k)
 
     def scatter(g, d, target):
         return (
@@ -126,6 +174,11 @@
             send_sem=x_s.at[n], recv_sem=x_r.at[n],
             device_id={"head": across}, device_id_type=MESH)
 
+    def send_across(n):
+        to_sibling(n, 0).wait_recv()
+        xsend[n] = (pbuf[n, across].astype(jnp.float32) + sib[n, 0].astype(jnp.float32)).astype(jnp.bfloat16)
+        to_across(n).start()
+
     barrier = pltpu.get_barrier_semaphore()
     for d in range(1, heads):
         pl.semaphore_signal(barrier, inc=1, device_id={"head": lax.rem(h + d, heads)}, device_id_type=MESH)
@@ -143,8 +196,7 @@
     def _(g):
         for d in (2, 1, 3):
             a2a(g, d, h, lax.rem(h + d, heads)).start()
-        qbuf[g, c, pl.ds(pl.multiple_of(h * rows, rows), rows), :] = q_ref[
-            :, pl.ds(pl.multiple_of(h * hg + g * cw, cw), cw)]
+        own_copy(g).start()
 
     @pl.loop(0, ncols)
     def _(n):
@@ -154,24 +206,38 @@
         bias[:, i * 128:(i + 1) * 128] = jnp.full(
             (8, 128), jnp.where(kept_ref[i] > 0, 0.0, -jnp.inf), jnp.float32)
 
+    exchanged(0)
+    for d in (2, 1, 3):
+        gather(d, c, lax.rem(c + d, ctxs)).start()
+    stage(1)
+    stage(2)
+
+    ones = jnp.ones((kbuf.shape[1], HD), jnp.bfloat16)
+    lane = lax.broadcasted_iota(jnp.int32, (2 * block, HD), 1)
+
     @pl.loop(0, groups)
     def _(g):
-        for d in range(1, heads):
-            a2a(g, d, lax.rem(h + heads - d, heads), h).wait_recv()
-        for d in range(1, ctxs):
-            gather(g, d, c, lax.rem(c + d, ctxs)).start()
-
-    ones = jnp.ones((kbuf.shape[1], HD), jnp.bfloat16)
-    lane = lax.broadcasted_iota(jnp.int32, (2 * block, HD), 1)
-
-    @pl.loop(0, groups)
-    def _(g):
-        for d in range(1, ctxs):
-            gather(g, d, lax.rem(c + ctxs - d, ctxs), c).wait_recv()
+        @pl.when(g == 0)
+        def _():
+            for d in range(1, ctxs):
+                gather(d, lax.rem(c + ctxs - d, ctxs), c).wait_recv()
+
+        @pl.when(jnp.logical_and(g > 0, c == last))
+        def _():
+            for k in range(last):
+                up(g, k, last - 1 - k).wait_recv()
+
+        @pl.when(jnp.logical_and(g > 0, c == 0))
+        def _():
+            for k in range(last):
+                down(g, k, 1 + k).wait_recv()
+
         for copy in kv_copies(g):
             copy.wait()
         stats = [jnp.zeros((2 * block, HD), jnp.float32) for _ in range(ctxs // 2)]
         for j in range(per):
+            if j == 1:
+                stage(g + 3)
             cols = slice(j * HD, (j + 1) * HD)
             key_head = kbuf[g, :, cols]
             value_head = jnp.concatenate([vbuf[g, :, cols], ones], axis=1)
@@ -223,11 +289,11 @@
         for i in range(2):
             to_sibling(n, i).start()
 
-    @pl.loop(0, ncols)
-    def _(n):
-        to_sibling(n, 0).wait_recv()
-        xsend[n] = (pbuf[n, across].astype(jnp.float32) + sib[n, 0].astype(jnp.float32)).astype(jnp.bfloat16)
-        to_across(n).start()
+        @pl.when(n > 0)
+        def _():
+            send_across(n - 1)
+
+    send_across(ncols - 1)
 
     for n in range(ncols):
         to_sibling(n, 1).wait_recv()
@@ -240,10 +306,21 @@
     def _(g):
         for d in range(1, heads):
             a2a(g, d, h, lax.rem(h + d, heads)).wait_send()
+        for k in range(last):
+            @pl.when(jnp.logical_and(g > 0, jnp.logical_and(c < last, c >= k)))
+            def _():
+                up(g, k, c - k).wait_send()
+
+            @pl.when(jnp.logical_and(g > 0, jnp.logical_and(c > 0, c + k <= last)))
+            def _():
+                down(g, k, c + k).wait_send()
+
         for d in range(1, ctxs):
-            gather(g, d, c, lax.rem(c + d, ctxs)).wait_send()
             for copy in scatter(g, d, lax.rem(c + d, ctxs)):
                 copy.wait_send()
+
+    for d in range(1, ctxs):
+        gather(d, c, lax.rem(c + d, ctxs)).wait_send()
 
     @pl.loop(0, ncols)
     def _(n):
@@ -267,7 +344,7 @@
     return pl.pallas_call(
         kernel,
         out_shape=jax.ShapeDtypeStruct((rows, width), bf),
-        in_specs=[vmem, hbm, hbm, pl.BlockSpec(memory_space=pltpu.SMEM), hbm],
+        in_specs=[hbm, hbm, hbm, pl.BlockSpec(memory_space=pltpu.SMEM), hbm],
         out_specs=vmem,
         scratch_shapes=[
             pltpu.VMEM((groups, key_count, cw), bf),
@@ -284,9 +361,11 @@
             pltpu.VMEM((ncols, 2, rows, nw), bf),
             pltpu.VMEM((ncols, rows, nw), bf),
             pltpu.VMEM((ncols, rows, nw), bf),
-            dma((2, groups)), dma((ncols,)),
+            dma((2, groups)), dma((ncols,)), dma((groups,)),
+            dma((groups, ctxs - 1)), dma((groups, ctxs - 1)),
+            dma((groups, ctxs - 1)), dma((groups, ctxs - 1)),
             dma((groups, 3)), dma((groups, 3)),
-            dma((groups, ctxs - 1)), dma((groups, ctxs - 1)),
+            dma((ctxs - 1,)), dma((ctxs - 1,)),
             dma((groups, ctxs - 1)), dma((groups, ctxs - 1)),
             dma((groups, ctxs - 1)), dma((groups, ctxs - 1)),
             dma((ncols, 2)), dma((ncols, 2)),

time: 98 us -> 85.1 us (0.87)
  Pallas kernels: 96 us -> 83.1 us
    pallas_call x1, Pallas kernels: 96 us -> 83.1 us  [fused_shards(): pl.pallas_call(kernel, out_shape=jax.ShapeDtypeStruct((rows, width), bf),...]
where the time goes in v2:
time: 85.1 us; the launch traced here: 84.9 us
  Pallas kernels  83.1 us (98%)
  local copies, waits for them, and re-layouts  1.77 us (2%)
    pallas_call x1, Pallas kernels, fused_shards(): pl.pallas_call(kernel, out_shape=jax.ShapeDtypeStruct((rows, width), bf),...  83.1 us
    unnamed x1, local copies, waits for them, and re-layouts  1.77 us

profile of v2, /device:TPU:0, one launch (start us, length us, event | category | flops | bytes accessed | tf_op | source)
XLA Modules:
  0.0 84.9 jit_solution(18334145765845182531)
XLA Ops:
  0.0 83.1 %attention.1 = bf16[32,6144]{1,0:T(8,128)(2,1)} custom-call(bf16[32,6144]{1,0:T(8,128)(2,1)} %q_hbm.1, bf16[2048,1536]{1,0:T(8,128)(2,1)} %k_hbm.1, bf16[2048,1536]{1,0:T(8,128)(2,1)} %v_hbm.1, s32[16]{0:T(128)} %kept_ref.1, bf16[1536,6144]{1,0:T(8,128)(2,1)} %w_hbm.1), custom_call_target="tpu_custom_call" | custom-call | flops 8858370048 | bytes 31457280 | tf_op jit(solution)/shard_map/attention/pallas_call | solution.py:344
  83.1 1.8 %copy.7 = bf16[32,6144]{1,0:T(8,128)(2,1)} copy(bf16[32,6144]{1,0:T(8,128)(2,1)} %attention.1) | data formatting | bytes 786432

commit v3 on v2

--- a/solution.py
+++ b/solution.py
@@ -62,8 +62,9 @@
 
 def kernel(
     q_hbm, k_hbm, v_hbm, kept_ref, w_hbm, out_ref,
-    kbuf, vbuf, wbuf, qbuf, abuf, sbuf, rbuf, srbuf, bias, att, pbuf, sib, xsend, xrecv,
-    kv_sem, w_sem, own_sem, up_s, up_r, dn_s, dn_r, a2a_s, a2a_r, ag_s, ag_r, rs_s, rs_r, st_s, st_r, sib_s, sib_r, x_s, x_r,
+    kbuf, vbuf, wbuf, qbuf, abuf, sbuf, rbuf, srbuf, dbuf, dlog, ubuf, ulog, bias, att, pbuf, sib, xsend, xrecv,
+    kv_sem, w_sem, own_sem, up_s, up_r, dn_s, dn_r, a2a_s, a2a_r, ag_s, ag_r, rs_s, rs_r, st_s, st_r,
+    pd_s, pd_r, pu_s, pu_r, sib_s, sib_r, x_s, x_r,
 ):
     heads, ctxs = 4, qbuf.shape[1]
     groups, _, block, cw = qbuf.shape
@@ -71,6 +72,7 @@
     hg = groups * cw
     per = cw // HD
     ncols, _, _, nw = pbuf.shape
+    last = ctxs - 1
     h = lax.axis_index("head")
     c = lax.axis_index("ctx")
 
@@ -115,8 +117,6 @@
             send_sem=dn_s.at[g, k], recv_sem=dn_r.at[g, k],
             device_id={"ctx": lax.rem(c + ctxs - 1, ctxs)}, device_id_type=MESH)
 
-    last = ctxs - 1
-
     def exchanged(g):
         own_copy(g).wait()
         for d in range(1, heads):
@@ -146,17 +146,94 @@
                     exchanged(g)
                 hop(g, k)
 
-    def scatter(g, d, target):
+    def scatter(d, target):
         return (
             pltpu.make_async_remote_copy(
-                src_ref=abuf.at[g, target], dst_ref=rbuf.at[g, d - 1],
-                send_sem=rs_s.at[g, d - 1], recv_sem=rs_r.at[g, d - 1],
+                src_ref=abuf.at[groups - 1, target], dst_ref=rbuf.at[d - 1],
+                send_sem=rs_s.at[d - 1], recv_sem=rs_r.at[d - 1],
                 device_id={"ctx": target}, device_id_type=MESH),
             pltpu.make_async_remote_copy(
-                src_ref=sbuf.at[g, target], dst_ref=srbuf.at[g, d - 1],
-                send_sem=st_s.at[g, d - 1], recv_sem=st_r.at[g, d - 1],
+                src_ref=sbuf.at[groups - 1, target], dst_ref=srbuf.at[d - 1],
+                send_sem=st_s.at[d - 1], recv_sem=st_r.at[d - 1],
                 device_id={"ctx": target}, device_id_type=MESH),
         )
+
+    def part_down(g, b):
+        target = lax.rem(c + ctxs - 1, ctxs)
+        return (
+            pltpu.make_async_remote_copy(
+                src_ref=sbuf.at[g, b], dst_ref=dlog.at[g, b],
+                send_sem=pd_s.at[1, g, b], recv_sem=pd_r.at[1, g, b],
+                device_id={"ctx": target}, device_id_type=MESH),
+            pltpu.make_async_remote_copy(
+                src_ref=abuf.at[g, b], dst_ref=dbuf.at[g, b],
+                send_sem=pd_s.at[0, g, b], recv_sem=pd_r.at[0, g, b],
+                device_id={"ctx": target}, device_id_type=MESH),
+        )
+
+    def part_up(g, b):
+        target = lax.rem(c + 1, ctxs)
+        return (
+            pltpu.make_async_remote_copy(
+                src_ref=sbuf.at[g, b], dst_ref=ulog.at[g, b],
+                send_sem=pu_s.at[1, g, b], recv_sem=pu_r.at[1, g, b],
+                device_id={"ctx": target}, device_id_type=MESH),
+            pltpu.make_async_remote_copy(
+                src_ref=abuf.at[g, b], dst_ref=ubuf.at[g, b],
+                send_sem=pu_s.at[0, g, b], recv_sem=pu_r.at[0, g, b],
+                device_id={"ctx": target}, device_id_type=MESH),
+        )
+
+    def merge(g, b, part, log):
+        mine, other = sbuf[g, b], log[g, b]
+        top = jnp.maximum(mine, other)
+        weights = jnp.exp2(mine - top), jnp.exp2(other - top)
+        total = weights[0] + weights[1]
+        sbuf[g, b] = top + jnp.log2(total)
+        columns = jnp.concatenate(
+            [weights[0] / total, weights[1] / total, jnp.zeros((HD - 16, block), jnp.float32)], axis=0).T
+        for j in range(per):
+            cols = slice(j * HD, (j + 1) * HD)
+            abuf[g, b, :, cols] = (
+                columns[:, j:j + 1] * abuf[g, b, :, cols].astype(jnp.float32)
+                + columns[:, 8 + j:9 + j] * part[g, b, :, cols].astype(jnp.float32)
+            ).astype(jnp.bfloat16)
+
+    def part_stage(g, s):
+        @pl.when(c == last - s)
+        def _():
+            for b in range(last - s):
+                if s:
+                    for copy in part_down(g, b):
+                        copy.wait_recv()
+                    merge(g, b, dbuf, dlog)
+                for copy in part_down(g, b):
+                    copy.start()
+
+        @pl.when(c == s)
+        def _():
+            for b in range(last, s, -1):
+                if s:
+                    for copy in part_up(g, b):
+                        copy.wait_recv()
+                    merge(g, b, ubuf, ulog)
+                for copy in part_up(g, b):
+                    copy.start()
+
+    def part_final(g):
+        @pl.when(c < last)
+        def _():
+            for copy in part_down(g, c):
+                copy.wait_recv()
+            merge(g, c, dbuf, dlog)
+
+        @pl.when(c > 0)
+        def _():
+            for copy in part_up(g, c):
+                copy.wait_recv()
+            merge(g, c, ubuf, ulog)
+
+        att[g] = abuf[g, c]
 
     sibling = h + 1 - 2 * lax.rem(h, 2)
     across = lax.rem(h + 2, 4)
@@ -257,27 +334,49 @@
         for t in range(ctxs // 2):
             for u in range(2):
                 sbuf[g, 2 * t + u] = stats[t][u * block:(u + 1) * block].T[0:8, :]
-        for d in range(1, ctxs):
-            for copy in scatter(g, d, lax.rem(c + d, ctxs)):
-                copy.start()
-
-    @pl.loop(0, groups)
-    def _(g):
-        for d in range(1, ctxs):
-            for copy in scatter(g, d, lax.rem(c + d, ctxs)):
-                copy.wait_recv()
-        logs = jnp.concatenate(
-            [sbuf[g, c]] + [srbuf[g, d] for d in range(ctxs - 1)]
-            + [jnp.zeros((HD - 8 * ctxs, block), jnp.float32)], axis=0).T
-        parts = [abuf[g, c]] + [rbuf[g, d] for d in range(ctxs - 1)]
-        for j in range(per):
-            own = [logs[:, 8 * i + j:8 * i + j + 1] for i in range(ctxs)]
-            top = functools.reduce(jnp.maximum, own)
-            weights = [jnp.exp2(x - top) for x in own]
-            total = functools.reduce(jnp.add, weights)
-            value = functools.reduce(jnp.add, [
-                w * x[:, j * HD:(j + 1) * HD].astype(jnp.float32) for w, x in zip(weights, parts)])
-            att[g, :, j * HD:(j + 1) * HD] = (value / total).astype(jnp.bfloat16)
+
+        @pl.when(g < groups - 1)
+        def _():
+            part_stage(g, 0)
+
+        @pl.when(g == groups - 1)
+        def _():
+            for d in (2, 1, 3):
+                for copy in scatter(d, lax.rem(c + d, ctxs)):
+                    copy.start()
+
+        @pl.when(g >= 1)
+        def _():
+            part_stage(g - 1, 1)
+
+        @pl.when(g >= 2)
+        def _():
+            part_stage(g - 2, 2)
+
+        @pl.when(g >= 3)
+        def _():
+            part_final(g - 3)
+
+    part_stage(groups - 2, 2)
+    part_final(groups - 3)
+    part_final(groups - 2)
+
+    for d in range(1, ctxs):
+        for copy in scatter(d, lax.rem(c + d, ctxs)):
+            copy.wait_recv()
+    final = groups - 1
+    logs = jnp.concatenate(
+        [sbuf[final, c]] + [srbuf[d] for d in range(ctxs - 1)]
+        + [jnp.zeros((HD - 8 * ctxs, block), jnp.float32)], axis=0).T
+    for j in range(per):
+        cols = slice(j * HD, (j + 1) * HD)
+        own = [logs[:, 8 * i + j:8 * i + j + 1] for i in range(ctxs)]
+        top = functools.reduce(jnp.maximum, own)
+        weights = [jnp.exp2(x - top) for x in own]
+        total = functools.reduce(jnp.add, weights)
+        parts = [abuf[final, c, :, cols]] + [rbuf[d, :, cols] for d in range(ctxs - 1)]
+        value = functools.reduce(jnp.add, [w * x.astype(jnp.float32) for w, x in zip(weights, parts)])
+        att[final, :, cols] = (value / total).astype(jnp.bfloat16)
 
     @pl.loop(0, ncols)
     def _(n):
@@ -315,12 +414,21 @@
             def _():
                 down(g, k, c + k).wait_send()
 
-        for d in range(1, ctxs):
-            for copy in scatter(g, d, lax.rem(c + d, ctxs)):
-                copy.wait_send()
+        for b in range(ctxs):
+            @pl.when(jnp.logical_and(g < groups - 1, b < c))
+            def _():
+                for copy in part_down(g, b):
+                    copy.wait_send()
+
+            @pl.when(jnp.logical_and(g < groups - 1, b > c))
+            def _():
+                for copy in part_up(g, b):
+                    copy.wait_send()
 
     for d in range(1, ctxs):
         gather(d, c, lax.rem(c + d, ctxs)).wait_send()
+        for copy in scatter(d, lax.rem(c + d, ctxs)):
+            copy.wait_send()
 
     @pl.loop(0, ncols)
     def _(n):
@@ -353,8 +461,12 @@
             pltpu.VMEM((groups, ctxs, block, cw), bf),
             pltpu.VMEM((groups, ctxs, block, cw), bf),
             pltpu.VMEM((groups, ctxs, 8, block), f32),
-            pltpu.VMEM((groups, ctxs - 1, block, cw), bf),
-            pltpu.VMEM((groups, ctxs - 1, 8, block), f32),
+            pltpu.VMEM((ctxs - 1, block, cw), bf),
+            pltpu.VMEM((ctxs - 1, 8, block), f32),
+            pltpu.VMEM((groups, ctxs, block, cw), bf),
+            pltpu.VMEM((groups, ctxs, 8, block), f32),
+            pltpu.VMEM((groups, ctxs, block, cw), bf),
+            pltpu.VMEM((groups, ctxs, 8, block), f32),
             pltpu.VMEM((8, key_count), f32),
             pltpu.VMEM((groups, block, cw), bf),
             pltpu.VMEM((ncols, 4, rows, nw), bf),
@@ -366,8 +478,10 @@
             dma((groups, ctxs - 1)), dma((groups, ctxs - 1)),
             dma((groups, 3)), dma((groups, 3)),
             dma((ctxs - 1,)), dma((ctxs - 1,)),
-            dma((groups, ctxs - 1)), dma((groups, ctxs - 1)),
-            dma((groups, ctxs - 1)), dma((groups, ctxs - 1)),
+            dma((ctxs - 1,)), dma((ctxs - 1,)),
+            dma((ctxs - 1,)), dma((ctxs - 1,)),
+            dma((2, groups, ctxs)), dma((2, groups, ctxs)),
+            dma((2, groups, ctxs)), dma((2, groups, ctxs)),
             dma((ncols, 2)), dma((ncols, 2)),
             dma((ncols,)), dma((ncols,)),
         ],

time: 85.1 us -> 82.2 us (0.966)
  Pallas kernels: 83.1 us -> 80.3 us
    pallas_call x1, Pallas kernels: 83.1 us -> 80.3 us  [fused_shards(): pl.pallas_call(kernel, out_shape=jax.ShapeDtypeStruct((rows, width), bf),...]
where the time goes in v3:
time: 82.2 us; the launch traced here: 82 us
  Pallas kernels  80.3 us (98%)
  local copies, waits for them, and re-layouts  1.77 us (2%)
    pallas_call x1, Pallas kernels, fused_shards(): pl.pallas_call(kernel, out_shape=jax.ShapeDtypeStruct((rows, width), bf),...  80.3 us
    unnamed x1, local copies, waits for them, and re-layouts  1.77 us

profile of v3, /device:TPU:0, one launch (start us, length us, event | category | flops | bytes accessed | tf_op | source)
XLA Modules:
  0.0 82.0 jit_solution(13352003343065166896)
XLA Ops:
  0.0 80.3 %attention.1 = bf16[32,6144]{1,0:T(8,128)(2,1)} custom-call(bf16[32,6144]{1,0:T(8,128)(2,1)} %q_hbm.1, bf16[2048,1536]{1,0:T(8,128)(2,1)} %k_hbm.1, bf16[2048,1536]{1,0:T(8,128)(2,1)} %v_hbm.1, s32[16]{0:T(128)} %kept_ref.1, bf16[1536,6144]{1,0:T(8,128)(2,1)} %w_hbm.1), custom_call_target="tpu_custom_call" | custom-call | flops 8858370048 | bytes 31457280 | tf_op jit(solution)/shard_map/attention/pallas_call | solution.py:452
  80.3 1.8 %copy.7 = bf16[32,6144]{1,0:T(8,128)(2,1)} copy(bf16[32,6144]{1,0:T(8,128)(2,1)} %attention.1) | data formatting | bytes 786432

commit v4 on v3

--- a/solution.py
+++ b/solution.py
@@ -9,6 +9,7 @@
 from jax.sharding import PartitionSpec as P
 
 HD = 128
+KC = 256
 MESH = pl.DeviceIdType.MESH
 SCALE2 = math.log2(math.e) / math.sqrt(HD)
 
@@ -63,6 +64,7 @@
 def kernel(
     q_hbm, k_hbm, v_hbm, kept_ref, w_hbm, out_ref,
     kbuf, vbuf, wbuf, qbuf, abuf, sbuf, rbuf, srbuf, dbuf, dlog, ubuf, ulog, bias, att, pbuf, sib, xsend, xrecv,
+    score_ref, prob_ref, top_ref,
     kv_sem, w_sem, own_sem, up_s, up_r, dn_s, dn_r, a2a_s, a2a_r, ag_s, ag_r, rs_s, rs_r, st_s, st_r,
     pd_s, pd_r, pu_s, pu_r, sib_s, sib_r, x_s, x_r,
 ):
@@ -289,7 +291,7 @@
     stage(1)
     stage(2)
 
-    ones = jnp.ones((kbuf.shape[1], HD), jnp.bfloat16)
+    ones = jnp.ones((kbuf.shape[1] // 2, HD), jnp.bfloat16)
     lane = lax.broadcasted_iota(jnp.int32, (2 * block, HD), 1)
 
     @pl.loop(0, groups)
@@ -311,26 +313,50 @@
 
         for copy in kv_copies(g):
             copy.wait()
+        stage(g + 3)
         stats = [jnp.zeros((2 * block, HD), jnp.float32) for _ in range(ctxs // 2)]
-        for j in range(per):
-            if j == 1:
-                stage(g + 3)
-            cols = slice(j * HD, (j + 1) * HD)
-            key_head = kbuf[g, :, cols]
-            value_head = jnp.concatenate([vbuf[g, :, cols], ones], axis=1)
-            for t in range(ctxs // 2):
-                query = qbuf[g, 2 * t:2 * t + 2, :, cols].reshape(2 * block, HD)
-                scores = lax.dot_general(
-                    query, key_head, (((1,), (1,)), ((), ())),
-                    preferred_element_type=jnp.float32) + bias[0:1, :]
-                highest = jnp.max(scores, axis=1, keepdims=True)
-                probs = jnp.exp2((scores - highest) * SCALE2)
-                mixed = jnp.dot(
-                    probs.astype(jnp.bfloat16), value_head, preferred_element_type=jnp.float32)
+        units = [(j, t) for j in range(per) for t in range(ctxs // 2)]
+        key_count = kbuf.shape[1]
+        chunks = key_count // KC
+        tops = {}
+        for u in range(len(units) + 1):
+            mixed = None
+            if u < len(units):
+                j, t = units[u]
+                query = qbuf[g, 2 * t:2 * t + 2, :, j * HD:(j + 1) * HD].reshape(2 * block, HD)
+                running = None
+            for kc in range(chunks):
+                keys = slice(kc * KC, (kc + 1) * KC)
+                if u < len(units):
+                    scores = lax.dot_general(
+                        query, kbuf[g, keys, j * HD:(j + 1) * HD], (((1,), (1,)), ((), ())),
+                        preferred_element_type=jnp.float32) + bias[0:1, keys]
+                    score_ref[u % 2, :, keys] = scores
+                    for i in range(KC // HD):
+                        piece = scores[:, i * HD:(i + 1) * HD]
+                        running = piece if running is None else jnp.maximum(running, piece)
+                if u > 0:
+                    pj, pt = units[u - 1]
+                    for i in range(KC // HD):
+                        cols = slice(kc * KC + i * HD, kc * KC + (i + 1) * HD)
+                        prob_ref[(u - 1) % 2, :, cols] = jnp.exp2(
+                            (score_ref[(u - 1) % 2, :, cols] - top_ref[(u - 1) % 2]) * SCALE2
+                        ).astype(jnp.bfloat16)
+                    if (kc + 1) % (chunks // 2) == 0:
+                        span = slice((kc + 1) * KC - key_count // 2, (kc + 1) * KC)
+                        value = jnp.concatenate([vbuf[g, span, pj * HD:(pj + 1) * HD], ones], axis=1)
+                        part = jnp.dot(
+                            prob_ref[(u - 1) % 2, :, span], value, preferred_element_type=jnp.float32)
+                        mixed = part if mixed is None else mixed + part
+            if u > 0:
                 normal = mixed[:, HD:]
-                abuf[g, 2 * t:2 * t + 2, :, cols] = (
+                abuf[g, 2 * pt:2 * pt + 2, :, pj * HD:(pj + 1) * HD] = (
                     (mixed[:, :HD] / normal).astype(jnp.bfloat16).reshape(2, block, HD))
-                stats[t] = jnp.where(lane == j, highest * SCALE2 + jnp.log2(normal), stats[t])
+                stats[pt] = jnp.where(
+                    lane == pj, top_ref[(u - 1) % 2] * SCALE2 + jnp.log2(normal), stats[pt])
+            if u < len(units):
+                top_ref[u % 2] = jnp.broadcast_to(
+                    jnp.max(running, axis=1, keepdims=True), (2 * block, HD))
         for t in range(ctxs // 2):
             for u in range(2):
                 sbuf[g, 2 * t + u] = stats[t][u * block:(u + 1) * block].T[0:8, :]
@@ -473,6 +499,9 @@
             pltpu.VMEM((ncols, 2, rows, nw), bf),
             pltpu.VMEM((ncols, rows, nw), bf),
             pltpu.VMEM((ncols, rows, nw), bf),
+            pltpu.VMEM((2, 2 * block, key_count), f32),
+            pltpu.VMEM((2, 2 * block, key_count), bf),
+            pltpu.VMEM((2, 2 * block, HD), f32),
             dma((2, groups)), dma((ncols,)), dma((groups,)),
             dma((groups, ctxs - 1)), dma((groups, ctxs - 1)),
             dma((groups, ctxs - 1)), dma((groups, ctxs - 1)),
@@ -486,7 +515,7 @@
             dma((ncols,)), dma((ncols,)),
         ],
         compiler_params=pltpu.CompilerParams(
-            collective_id=0, has_side_effects=True, vmem_limit_bytes=60 * 2**20),
+            collective_id=0, has_side_effects=True, vmem_limit_bytes=62 * 2**20),
         cost_estimate=pl.CostEstimate(
             flops=4 * ctxs * block * key_count * hg + 2 * block * hg * width,
             bytes_accessed=2 * (2 * key_count * hg + hg * width),

time: 82.2 us -> 79.5 us (0.967)
  Pallas kernels: 80.3 us -> 77.5 us
    pallas_call x1, Pallas kernels: 80.3 us -> 77.5 us  [fused_shards(): pl.pallas_call(kernel, out_shape=jax.ShapeDtypeStruct((rows, width), bf),...]
where the time goes in v4:
time: 79.5 us; the launch traced here: 79.3 us
  Pallas kernels  77.5 us (97%)
  local copies, waits for them, and re-layouts  1.77 us (2%)
    pallas_call x1, Pallas kernels, fused_shards(): pl.pallas_call(kernel, out_shape=jax.ShapeDtypeStruct((rows, width), bf),...  77.5 us
    unnamed x1, local copies, waits for them, and re-layouts  1.77 us

profile of v4, /device:TPU:0, one launch (start us, length us, event | category | flops | bytes accessed | tf_op | source)
XLA Modules:
  0.0 79.3 jit_solution(4233615617344346635)
XLA Ops:
  0.0 77.5 %attention.1 = bf16[32,6144]{1,0:T(8,128)(2,1)} custom-call(bf16[32,6144]{1,0:T(8,128)(2,1)} %q_hbm.1, bf16[2048,1536]{1,0:T(8,128)(2,1)} %k_hbm.1, bf16[2048,1536]{1,0:T(8,128)(2,1)} %v_hbm.1, s32[16]{0:T(128)} %kept_ref.1, bf16[1536,6144]{1,0:T(8,128)(2,1)} %w_hbm.1), custom_call_target="tpu_custom_call" | custom-call | flops 8858370048 | bytes 31457280 | tf_op jit(solution)/shard_map/attention/pallas_call | solution.py:478
  77.5 1.8 %copy.7 = bf16[32,6144]{1,0:T(8,128)(2,1)} copy(bf16[32,6144]{1,0:T(8,128)(2,1)} %attention.1) | data formatting | bytes 786432

commit v5 on v4

--- a/solution.py
+++ b/solution.py
@@ -69,11 +69,12 @@
     pd_s, pd_r, pu_s, pu_r, sib_s, sib_r, x_s, x_r,
 ):
     heads, ctxs = 4, qbuf.shape[1]
-    groups, _, block, cw = qbuf.shape
-    rows = q_hbm.shape[0]
+    groups = kbuf.shape[0]
+    slots, _, block, cw = qbuf.shape
+    rows = q_hbm.shape[0] // 2
     hg = groups * cw
     per = cw // HD
-    ncols, _, _, nw = pbuf.shape
+    ncols, _, nw = wbuf.shape
     last = ctxs - 1
     h = lax.axis_index("head")
     c = lax.axis_index("ctx")
@@ -89,16 +90,22 @@
         cols = pl.ds(pl.multiple_of(n * nw, nw), nw)
         return pltpu.make_async_copy(w_hbm.at[:, cols], wbuf.at[n], w_sem.at[n])
 
+    def query_part(i, target):
+        first = target * hg + lax.rem(i, groups) * cw
+        return q_hbm.at[
+            pl.ds(pl.multiple_of(lax.div(i, groups) * rows, rows), rows),
+            pl.ds(pl.multiple_of(first, cw), cw)]
+
     def a2a(g, d, sender, target):
         return pltpu.make_async_remote_copy(
-            src_ref=q_hbm.at[:, pl.ds(pl.multiple_of(target * hg + g * cw, cw), cw)],
+            src_ref=query_part(g, target),
             dst_ref=qbuf.at[g, c, pl.ds(pl.multiple_of(sender * rows, rows), rows), :],
             send_sem=a2a_s.at[g, d - 1], recv_sem=a2a_r.at[g, d - 1],
             device_id={"head": target}, device_id_type=MESH)
 
     def own_copy(g):
         return pltpu.make_async_copy(
-            q_hbm.at[:, pl.ds(pl.multiple_of(h * hg + g * cw, cw), cw)],
+            query_part(g, h),
             qbuf.at[g, c, pl.ds(pl.multiple_of(h * rows, rows), rows), :], own_sem.at[g])
 
     def gather(d, sender, target):
@@ -140,7 +147,7 @@
     def stage(s):
         for k in range(last):
             g = s - k
-            inside = jnp.logical_and(g >= 1, g < groups)
+            inside = jnp.logical_and(g >= 1, g < slots)
 
             @pl.when(inside)
             def _():
@@ -151,11 +158,11 @@
     def scatter(d, target):
         return (
             pltpu.make_async_remote_copy(
-                src_ref=abuf.at[groups - 1, target], dst_ref=rbuf.at[d - 1],
+                src_ref=abuf.at[slots - 1, target], dst_ref=rbuf.at[d - 1],
                 send_sem=rs_s.at[d - 1], recv_sem=rs_r.at[d - 1],
                 device_id={"ctx": target}, device_id_type=MESH),
             pltpu.make_async_remote_copy(
-                src_ref=sbuf.at[groups - 1, target], dst_ref=srbuf.at[d - 1],
+                src_ref=sbuf.at[slots - 1, target], dst_ref=srbuf.at[d - 1],
                 send_sem=st_s.at[d - 1], recv_sem=st_r.at[d - 1],
                 device_id={"ctx": target}, device_id_type=MESH),
         )
@@ -193,7 +200,7 @@
         total = weights[0] + weights[1]
         sbuf[g, b] = top + jnp.log2(total)
         columns = jnp.concatenate(
-            [weights[0] / total, weights[1] / total, jnp.zeros((HD - 16, block), jnp.float32)], axis=0).T
+            [weights[0] / total, weights[1] / total, jnp.zeros((HD - 16, HD), jnp.float32)], axis=0).T[0:block]
         for j in range(per):
             cols = slice(j * HD, (j + 1) * HD)
             abuf[g, b, :, cols] = (
@@ -235,7 +242,22 @@
                 copy.wait_recv()
             merge(g, c, ubuf, ulog)
 
-        att[g] = abuf[g, c]
+        att[lax.div(g, groups), :, pl.ds(pl.multiple_of(lax.rem(g, groups) * cw, cw), cw)] = abuf[g, c]
+
+    def project(m):
+        n = lax.rem(m, ncols)
+        total = jnp.dot(att[lax.div(m, ncols)], wbuf[n], preferred_element_type=jnp.float32)
+        pbuf[m] = total.astype(jnp.bfloat16).reshape(heads, rows, nw)
+        for i in range(2):
+            to_sibling(m, i).start()
+
+    def finish(m):
+        to_sibling(m, 1).wait_recv()
+        to_across(m).wait_recv()
+        half, n = divmod(m, ncols)
+        out_ref[half * rows:(half + 1) * rows, n * nw:(n + 1) * nw] = (
+            pbuf[m, h].astype(jnp.float32) + sib[m, 1].astype(jnp.float32)
+            + xrecv[m].astype(jnp.float32)).astype(jnp.bfloat16)
 
     sibling = h + 1 - 2 * lax.rem(h, 2)
     across = lax.rem(h + 2, 4)
@@ -271,7 +293,7 @@
 
     pl.semaphore_wait(barrier, heads + ctxs - 2)
 
-    @pl.loop(0, groups)
+    @pl.loop(0, slots)
     def _(g):
         for d in (2, 1, 3):
             a2a(g, d, h, lax.rem(h + d, heads)).start()
@@ -292,10 +314,12 @@
     stage(2)
 
     ones = jnp.ones((kbuf.shape[1] // 2, HD), jnp.bfloat16)
-    lane = lax.broadcasted_iota(jnp.int32, (2 * block, HD), 1)
-
-    @pl.loop(0, groups)
+    lane = lax.broadcasted_iota(jnp.int32, (ctxs * block, HD), 1)
+
+    @pl.loop(0, slots)
     def _(g):
+        group = lax.rem(g, groups)
+
         @pl.when(g == 0)
         def _():
             for d in range(1, ctxs):
@@ -311,32 +335,34 @@
             for k in range(last):
                 down(g, k, 1 + k).wait_recv()
 
-        for copy in kv_copies(g):
-            copy.wait()
+        @pl.when(g < groups)
+        def _():
+            for copy in kv_copies(g):
+                copy.wait()
+
         stage(g + 3)
-        stats = [jnp.zeros((2 * block, HD), jnp.float32) for _ in range(ctxs // 2)]
-        units = [(j, t) for j in range(per) for t in range(ctxs // 2)]
+        stats = jnp.zeros((ctxs * block, HD), jnp.float32)
+        units = per
         key_count = kbuf.shape[1]
         chunks = key_count // KC
         tops = {}
-        for u in range(len(units) + 1):
+        for u in range(units + 1):
             mixed = None
-            if u < len(units):
-                j, t = units[u]
-                query = qbuf[g, 2 * t:2 * t + 2, :, j * HD:(j + 1) * HD].reshape(2 * block, HD)
+            if u < units:
+                query = qbuf[g, :, :, u * HD:(u + 1) * HD].reshape(ctxs * block, HD)
                 running = None
             for kc in range(chunks):
                 keys = slice(kc * KC, (kc + 1) * KC)
-                if u < len(units):
+                if u < units:
                     scores = lax.dot_general(
-                        query, kbuf[g, keys, j * HD:(j + 1) * HD], (((1,), (1,)), ((), ())),
+                        query, kbuf[group, keys, u * HD:(u + 1) * HD], (((1,), (1,)), ((), ())),
                         preferred_element_type=jnp.float32) + bias[0:1, keys]
                     score_ref[u % 2, :, keys] = scores
                     for i in range(KC // HD):
                         piece = scores[:, i * HD:(i + 1) * HD]
                         running = piece if running is None else jnp.maximum(running, piece)
                 if u > 0:
-                    pj, pt = units[u - 1]
+                    pj = u - 1
                     for i in range(KC // HD):
                         cols = slice(kc * KC + i * HD, kc * KC + (i + 1) * HD)
                         prob_ref[(u - 1) % 2, :, cols] = jnp.exp2(
@@ -344,56 +370,76 @@
                         ).astype(jnp.bfloat16)
                     if (kc + 1) % (chunks // 2) == 0:
                         span = slice((kc + 1) * KC - key_count // 2, (kc + 1) * KC)
-                        value = jnp.concatenate([vbuf[g, span, pj * HD:(pj + 1) * HD], ones], axis=1)
+                        value = jnp.concatenate([vbuf[group, span, pj * HD:(pj + 1) * HD], ones], axis=1)
                         part = jnp.dot(
                             prob_ref[(u - 1) % 2, :, span], value, preferred_element_type=jnp.float32)
                         mixed = part if mixed is None else mixed + part
             if u > 0:
                 normal = mixed[:, HD:]
-                abuf[g, 2 * pt:2 * pt + 2, :, pj * HD:(pj + 1) * HD] = (
-                    (mixed[:, :HD] / normal).astype(jnp.bfloat16).reshape(2, block, HD))
-                stats[pt] = jnp.where(
-                    lane == pj, top_ref[(u - 1) % 2] * SCALE2 + jnp.log2(normal), stats[pt])
-            if u < len(units):
+                abuf[g, :, :, pj * HD:(pj + 1) * HD] = (
+                    (mixed[:, :HD] / normal).astype(jnp.bfloat16).reshape(ctxs, block, HD))
+                stats = jnp.where(
+                    lane == pj, top_ref[(u - 1) % 2] * SCALE2 + jnp.log2(normal), stats)
+            if u < units:
                 top_ref[u % 2] = jnp.broadcast_to(
-                    jnp.max(running, axis=1, keepdims=True), (2 * block, HD))
-        for t in range(ctxs // 2):
-            for u in range(2):
-                sbuf[g, 2 * t + u] = stats[t][u * block:(u + 1) * block].T[0:8, :]
-
-        @pl.when(g < groups - 1)
+                    jnp.max(running, axis=1, keepdims=True), (ctxs * block, HD))
+        pad = jnp.zeros((HD - block, HD), jnp.float32)
+        for b in range(ctxs):
+            sbuf[g, b] = jnp.concatenate([stats[b * block:(b + 1) * block], pad], axis=0).T[0:8, :]
+
+        @pl.when(g < slots - 1)
         def _():
             part_stage(g, 0)
 
-        @pl.when(g == groups - 1)
+        @pl.when(g >= 3)
+        def _():
+            part_final(g - 3)
+
+        @pl.when(g >= 2)
+        def _():
+            part_stage(g - 2, 2)
+
+        @pl.when(g >= 1)
+        def _():
+            part_stage(g - 1, 1)
+
+        @pl.when(g == slots - 1)
         def _():
             for d in (2, 1, 3):
                 for copy in scatter(d, lax.rem(c + d, ctxs)):
                     copy.start()
 
-        @pl.when(g >= 1)
-        def _():
-            part_stage(g - 1, 1)
-
-        @pl.when(g >= 2)
-        def _():
-            part_stage(g - 2, 2)
-
-        @pl.when(g >= 3)
-        def _():
-            part_final(g - 3)
-
-    part_stage(groups - 2, 2)
-    part_final(groups - 3)
-    part_final(groups - 2)
+        begin = groups + 3
+        share = ncols // (slots - begin)
+
+        @pl.when(g == begin)
+        def _():
+            for n in range(ncols):
+                w_copy(n).wait()
+
+        @pl.when(g > begin)
+        def _():
+            for i in range(share):
+                send_across((g - begin - 1) * share + i)
+
+        @pl.when(g >= begin)
+        def _():
+            for i in range(share):
+                project((g - begin) * share + i)
+
+    part_stage(slots - 2, 2)
+    part_final(slots - 3)
+    for m in range(ncols - ncols // (groups - 3), ncols):
+        send_across(m)
+    part_final(slots - 2)
 
     for d in range(1, ctxs):
         for copy in scatter(d, lax.rem(c + d, ctxs)):
             copy.wait_recv()
-    final = groups - 1
+    final = slots - 1
     logs = jnp.concatenate(
         [sbuf[final, c]] + [srbuf[d] for d in range(ctxs - 1)]
-        + [jnp.zeros((HD - 8 * ctxs, block), jnp.float32)], axis=0).T
+        + [jnp.zeros((HD - 8 * ctxs, HD), jnp.float32)], axis=0).T[0:block]
     for j in range(per):
         cols = slice(j * HD, (j + 1) * HD)
         own = [logs[:, 8 * i + j:8 * i + j + 1] for i in range(ctxs)]
@@ -402,32 +448,23 @@
         total = functools.reduce(jnp.add, weights)
         parts = [abuf[final, c, :, cols]] + [rbuf[d, :, cols] for d in range(ctxs - 1)]
         value = functools.reduce(jnp.add, [w * x.astype(jnp.float32) for w, x in zip(weights, parts)])
-        att[final, :, cols] = (value / total).astype(jnp.bfloat16)
+        first = (groups - 1) * cw + j * HD
+        att[1, :, first:first + HD] = (value / total).astype(jnp.bfloat16)
 
     @pl.loop(0, ncols)
     def _(n):
-        w_copy(n).wait()
-        total = functools.reduce(jnp.add, [
-            jnp.dot(att[g], wbuf[n, g * cw:(g + 1) * cw, :], preferred_element_type=jnp.float32)
-            for g in range(groups)])
-        pbuf[n] = total.astype(jnp.bfloat16).reshape(heads, rows, nw)
-        for i in range(2):
-            to_sibling(n, i).start()
+        project(ncols + n)
 
         @pl.when(n > 0)
         def _():
-            send_across(n - 1)
-
-    send_across(ncols - 1)
-
-    for n in range(ncols):
-        to_sibling(n, 1).wait_recv()
-        to_across(n).wait_recv()
-        out_ref[:, n * nw:(n + 1) * nw] = (
-            pbuf[n, h].astype(jnp.float32) + sib[n, 1].astype(jnp.float32)
-            + xrecv[n].astype(jnp.float32)).astype(jnp.bfloat16)
-
-    @pl.loop(0, groups)
+            send_across(ncols + n - 1)
+
+    send_across(2 * ncols - 1)
+
+    for m in range(2 * ncols):
+        finish(m)
+
+    @pl.loop(0, slots)
     def _(g):
         for d in range(1, heads):
             a2a(g, d, h, lax.rem(h + d, heads)).wait_send()
@@ -441,12 +478,12 @@
                 down(g, k, c + k).wait_send()
 
         for b in range(ctxs):
-            @pl.when(jnp.logical_and(g < groups - 1, b < c))
+            @pl.when(jnp.logical_and(g < slots - 1, b < c))
             def _():
                 for copy in part_down(g, b):
                     copy.wait_send()
 
-            @pl.when(jnp.logical_and(g < groups - 1, b > c))
+            @pl.when(jnp.logical_and(g < slots - 1, b > c))
             def _():
                 for copy in part_up(g, b):
                     copy.wait_send()
@@ -456,7 +493,7 @@
         for copy in scatter(d, lax.rem(c + d, ctxs)):
             copy.wait_send()
 
-    @pl.loop(0, ncols)
+    @pl.loop(0, 2 * ncols)
     def _(n):
         to_sibling(n, 0).wait_send()
         to_sibling(n, 1).wait_send()
@@ -468,7 +505,8 @@
     key_count, hg = keys.shape
     cw = 2 * HD
     groups = hg // cw
-    block = 4 * rows
+    block = 2 * rows
+    slots = 2 * groups
     nw = 1024
     ncols = width // nw
     bf, f32 = jnp.bfloat16, jnp.float32
@@ -484,42 +522,42 @@
             pltpu.VMEM((groups, key_count, cw), bf),
             pltpu.VMEM((groups, key_count, cw), bf),
             pltpu.VMEM((ncols, hg, nw), bf),
-            pltpu.VMEM((groups, ctxs, block, cw), bf),
-            pltpu.VMEM((groups, ctxs, block, cw), bf),
-            pltpu.VMEM((groups, ctxs, 8, block), f32),
+            pltpu.VMEM((slots, ctxs, block, cw), bf),
+            pltpu.VMEM((slots, ctxs, block, cw), bf),
+            pltpu.VMEM((slots, ctxs, 8, HD), f32),
             pltpu.VMEM((ctxs - 1, block, cw), bf),
-            pltpu.VMEM((ctxs - 1, 8, block), f32),
-            pltpu.VMEM((groups, ctxs, block, cw), bf),
-            pltpu.VMEM((groups, ctxs, 8, block), f32),
-            pltpu.VMEM((groups, ctxs, block, cw), bf),
-            pltpu.VMEM((groups, ctxs, 8, block), f32),
+            pltpu.VMEM((ctxs - 1, 8, HD), f32),
+            pltpu.VMEM((slots, ctxs, block, cw), bf),
+            pltpu.VMEM((slots, ctxs, 8, HD), f32),
+            pltpu.VMEM((slots, ctxs, block, cw), bf),
+            pltpu.VMEM((slots, ctxs, 8, HD), f32),
             pltpu.VMEM((8, key_count), f32),
-            pltpu.VMEM((groups, block, cw), bf),
-            pltpu.VMEM((ncols, 4, rows, nw), bf),
-            pltpu.VMEM((ncols, 2, rows, nw), bf),
-            pltpu.VMEM((ncols, rows, nw), bf),
-            pltpu.VMEM((ncols, rows, nw), bf),
-            pltpu.VMEM((2, 2 * block, key_count), f32),
-            pltpu.VMEM((2, 2 * block, key_count), bf),
-            pltpu.VMEM((2, 2 * block, HD), f32),
-            dma((2, groups)), dma((ncols,)), dma((groups,)),
-            dma((groups, ctxs - 1)), dma((groups, ctxs - 1)),
-            dma((groups, ctxs - 1)), dma((groups, ctxs - 1)),
-            dma((groups, 3)), dma((groups, 3)),
+            pltpu.VMEM((2, block, hg), bf),
+            pltpu.VMEM((2 * ncols, 4, rows // 2, nw), bf),
+            pltpu.VMEM((2 * ncols, 2, rows // 2, nw), bf),
+            pltpu.VMEM((2 * ncols, rows // 2, nw), bf),
+            pltpu.VMEM((2 * ncols, rows // 2, nw), bf),
+            pltpu.VMEM((2, ctxs * block, key_count), f32),
+            pltpu.VMEM((2, ctxs * block, key_count), bf),
+            pltpu.VMEM((2, ctxs * block, HD), f32),
+            dma((2, groups)), dma((ncols,)), dma((slots,)),
+            dma((slots, ctxs - 1)), dma((slots, ctxs - 1)),
+            dma((slots, ctxs - 1)), dma((slots, ctxs - 1)),
+            dma((slots, 3)), dma((slots, 3)),
             dma((ctxs - 1,)), dma((ctxs - 1,)),
             dma((ctxs - 1,)), dma((ctxs - 1,)),
             dma((ctxs - 1,)), dma((ctxs - 1,)),
-            dma((2, groups, ctxs)), dma((2, groups, ctxs)),
-            dma((2, groups, ctxs)), dma((2, groups, ctxs)),
-            dma((ncols, 2)), dma((ncols, 2)),
-            dma((ncols,)), dma((ncols,)),
+            dma((2, slots, ctxs)), dma((2, slots, ctxs)),
+            dma((2, slots, ctxs)), dma((2, slots, ctxs)),
+            dma((2 * ncols, 2)), dma((2 * ncols, 2)),
+            dma((2 * ncols,)), dma((2 * ncols,)),
         ],
         compiler_params=pltpu.CompilerParams(
             collective_id=0, has_side_effects=True, vmem_limit_bytes=62 * 2**20),
         cost_estimate=pl.CostEstimate(
-            flops=4 * ctxs * block * key_count * hg + 2 * block * hg * width,
+            flops=8 * ctxs * block * key_count * hg + 4 * block * hg * width,
             bytes_accessed=2 * (2 * key_count * hg + hg * width),
-            transcendentals=ctxs * block * key_count * hg // HD),
+            transcendentals=2 * ctxs * block * key_count * hg // HD),
         name="attention",
     )(queries, keys, values, kept_rows, out_weight)
 
@@ -529,7 +567,7 @@
 
     def shards(queries, keys, values, kept_rows, out_weight):
         rows = queries.shape[0]
-        if heads == 4 and ctxs == 4 and rows == 32 and keys.shape[1] % (2 * HD) == 0:
+        if heads == 4 and ctxs == 4 and rows == 32 and keys.shape[1] == 12 * HD:
             return fused_shards(ctxs, queries, keys, values, kept_rows, out_weight)
         return general_shards(queries, keys, values, kept_rows, out_weight)
 

time: 79.5 us -> 86.9 us (1.093)
  Pallas kernels: 77.5 us -> 84.9 us
    pallas_call x1, Pallas kernels: 77.5 us -> 84.9 us  [fused_shards(): pl.pallas_call(kernel, out_shape=jax.ShapeDtypeStruct((rows, width), bf),...]
where the time goes in v5:
time: 86.9 us; the launch traced here: 86.7 us
  Pallas kernels  84.9 us (98%)
  local copies, waits for them, and re-layouts  1.77 us (2%)
    pallas_call x1, Pallas kernels, fused_shards(): pl.pallas_call(kernel, out_shape=jax.ShapeDtypeStruct((rows, width), bf),...  84.9 us
    unnamed x1, local copies, waits for them, and re-layouts  1.77 us

profile of v5, /device:TPU:0, one launch (start us, length us, event | category | flops | bytes accessed | tf_op | source)
XLA Modules:
  0.0 86.7 jit_solution(2846655153020629765)
XLA Ops:
  0.0 84.9 %attention.1 = bf16[32,6144]{1,0:T(8,128)(2,1)} custom-call(bf16[32,6144]{1,0:T(8,128)(2,1)} %q_hbm.1, bf16[2048,1536]{1,0:T(8,128)(2,1)} %k_hbm.1, bf16[2048,1536]{1,0:T(8,128)(2,1)} %v_hbm.1, s32[16]{0:T(128)} %kept_ref.1, bf16[1536,6144]{1,0:T(8,128)(2,1)} %w_hbm.1), custom_call_target="tpu_custom_call" | custom-call | flops 8858370048 | bytes 31457280 | tf_op jit(solution)/shard_map/attention/pallas_call | solution.py:516
  84.9 1.8 %copy.7 = bf16[32,6144]{1,0:T(8,128)(2,1)} copy(bf16[32,6144]{1,0:T(8,128)(2,1)} %attention.1) | data formatting | bytes 786432

commit v6 on v4

--- a/solution.py
+++ b/solution.py
@@ -10,6 +10,8 @@
 
 HD = 128
 KC = 256
+AHEAD = 2
+DIRECT = 3
 MESH = pl.DeviceIdType.MESH
 SCALE2 = math.log2(math.e) / math.sqrt(HD)
 
@@ -64,7 +66,7 @@
 def kernel(
     q_hbm, k_hbm, v_hbm, kept_ref, w_hbm, out_ref,
     kbuf, vbuf, wbuf, qbuf, abuf, sbuf, rbuf, srbuf, dbuf, dlog, ubuf, ulog, bias, att, pbuf, sib, xsend, xrecv,
-    score_ref, prob_ref, top_ref,
+    score_ref, prob_ref, top_ref, early,
     kv_sem, w_sem, own_sem, up_s, up_r, dn_s, dn_r, a2a_s, a2a_r, ag_s, ag_r, rs_s, rs_r, st_s, st_r,
     pd_s, pd_r, pu_s, pu_r, sib_s, sib_r, x_s, x_r,
 ):
@@ -75,6 +77,7 @@
     per = cw // HD
     ncols, _, _, nw = pbuf.shape
     last = ctxs - 1
+    merged = groups - DIRECT
     h = lax.axis_index("head")
     c = lax.axis_index("ctx")
 
@@ -101,10 +104,10 @@
             q_hbm.at[:, pl.ds(pl.multiple_of(h * hg + g * cw, cw), cw)],
             qbuf.at[g, c, pl.ds(pl.multiple_of(h * rows, rows), rows), :], own_sem.at[g])
 
-    def gather(d, sender, target):
+    def gather(g, d, sender, target):
         return pltpu.make_async_remote_copy(
-            src_ref=qbuf.at[0, sender], dst_ref=qbuf.at[0, sender],
-            send_sem=ag_s.at[d - 1], recv_sem=ag_r.at[d - 1],
+            src_ref=qbuf.at[g, sender], dst_ref=qbuf.at[g, sender],
+            send_sem=ag_s.at[g, d - 1], recv_sem=ag_r.at[g, d - 1],
             device_id={"ctx": target}, device_id_type=MESH)
 
     def up(g, k, part):
@@ -140,7 +143,7 @@
     def stage(s):
         for k in range(last):
             g = s - k
-            inside = jnp.logical_and(g >= 1, g < groups)
+            inside = jnp.logical_and(g >= AHEAD, g < groups)
 
             @pl.when(inside)
             def _():
@@ -148,15 +151,15 @@
                     exchanged(g)
                 hop(g, k)
 
-    def scatter(d, target):
+    def scatter(g, d, target):
         return (
             pltpu.make_async_remote_copy(
-                src_ref=abuf.at[groups - 1, target], dst_ref=rbuf.at[d - 1],
-                send_sem=rs_s.at[d - 1], recv_sem=rs_r.at[d - 1],
+                src_ref=abuf.at[g, target], dst_ref=rbuf.at[g - merged, d - 1],
+                send_sem=rs_s.at[g - merged, d - 1], recv_sem=rs_r.at[g - merged, d - 1],
                 device_id={"ctx": target}, device_id_type=MESH),
             pltpu.make_async_remote_copy(
-                src_ref=sbuf.at[groups - 1, target], dst_ref=srbuf.at[d - 1],
-                send_sem=st_s.at[d - 1], recv_sem=st_r.at[d - 1],
+                src_ref=sbuf.at[g, target], dst_ref=srbuf.at[g - merged, d - 1],
+                send_sem=st_s.at[g - merged, d - 1], recv_sem=st_r.at[g - merged, d - 1],
                 device_id={"ctx": target}, device_id_type=MESH),
         )
 
@@ -237,6 +240,23 @@
 
         att[g] = abuf[g, c]
 
+    def direct_final(g):
+        for d in range(1, ctxs):
+            for copy in scatter(g, d, lax.rem(c + d, ctxs)):
+                copy.wait_recv()
+        logs = jnp.concatenate(
+            [sbuf[g, c]] + [srbuf[g - merged, d] for d in range(ctxs - 1)]
+            + [jnp.zeros((HD - 8 * ctxs, block), jnp.float32)], axis=0).T
+        for j in range(per):
+            cols = slice(j * HD, (j + 1) * HD)
+            own = [logs[:, 8 * i + j:8 * i + j + 1] for i in range(ctxs)]
+            top = functools.reduce(jnp.maximum, own)
+            weights = [jnp.exp2(x - top) for x in own]
+            total = functools.reduce(jnp.add, weights)
+            parts = [abuf[g, c, :, cols]] + [rbuf[g - merged, d, :, cols] for d in range(ctxs - 1)]
+            value = functools.reduce(jnp.add, [w * x.astype(jnp.float32) for w, x in zip(weights, parts)])
+            att[g, :, cols] = (value / total).astype(jnp.bfloat16)
+
     sibling = h + 1 - 2 * lax.rem(h, 2)
     across = lax.rem(h + 2, 4)
     diagonal = lax.rem(sibling + 2, 4)
@@ -287,26 +307,30 @@
 
     exchanged(0)
     for d in (2, 1, 3):
-        gather(d, c, lax.rem(c + d, ctxs)).start()
-    stage(1)
-    stage(2)
+        gather(0, d, c, lax.rem(c + d, ctxs)).start()
+    exchanged(AHEAD)
+    hop(AHEAD, 0)
+    for g in range(1, AHEAD):
+        exchanged(g)
+        for d in (2, 1, 3):
+            gather(g, d, c, lax.rem(c + d, ctxs)).start()
 
     ones = jnp.ones((kbuf.shape[1] // 2, HD), jnp.bfloat16)
     lane = lax.broadcasted_iota(jnp.int32, (2 * block, HD), 1)
 
     @pl.loop(0, groups)
     def _(g):
-        @pl.when(g == 0)
+        @pl.when(g < AHEAD)
         def _():
             for d in range(1, ctxs):
-                gather(d, lax.rem(c + ctxs - d, ctxs), c).wait_recv()
-
-        @pl.when(jnp.logical_and(g > 0, c == last))
+                gather(g, d, lax.rem(c + ctxs - d, ctxs), c).wait_recv()
+
+        @pl.when(jnp.logical_and(g >= AHEAD, c == last))
         def _():
             for k in range(last):
                 up(g, k, last - 1 - k).wait_recv()
 
-        @pl.when(jnp.logical_and(g > 0, c == 0))
+        @pl.when(jnp.logical_and(g >= AHEAD, c == 0))
         def _():
             for k in range(last):
                 down(g, k, 1 + k).wait_recv()
@@ -361,55 +385,52 @@
             for u in range(2):
                 sbuf[g, 2 * t + u] = stats[t][u * block:(u + 1) * block].T[0:8, :]
 
-        @pl.when(g < groups - 1)
+        @pl.when(g < merged)
         def _():
             part_stage(g, 0)
 
-        @pl.when(g == groups - 1)
+        @pl.when(g >= merged)
         def _():
             for d in (2, 1, 3):
-                for copy in scatter(d, lax.rem(c + d, ctxs)):
+                for copy in scatter(g, d, lax.rem(c + d, ctxs)):
                     copy.start()
 
-        @pl.when(g >= 1)
-        def _():
-            part_stage(g - 1, 1)
-
-        @pl.when(g >= 2)
-        def _():
-            part_stage(g - 2, 2)
-
-        @pl.when(g >= 3)
-        def _():
-            part_final(g - 3)
-
-    part_stage(groups - 2, 2)
-    part_final(groups - 3)
-    part_final(groups - 2)
-
-    for d in range(1, ctxs):
-        for copy in scatter(d, lax.rem(c + d, ctxs)):
-            copy.wait_recv()
-    final = groups - 1
-    logs = jnp.concatenate(
-        [sbuf[final, c]] + [srbuf[d] for d in range(ctxs - 1)]
-        + [jnp.zeros((HD - 8 * ctxs, block), jnp.float32)], axis=0).T
-    for j in range(per):
-        cols = slice(j * HD, (j + 1) * HD)
-        own = [logs[:, 8 * i + j:8 * i + j + 1] for i in range(ctxs)]
-        top = functools.reduce(jnp.maximum, own)
-        weights = [jnp.exp2(x - top) for x in own]
-        total = functools.reduce(jnp.add, weights)
-        parts = [abuf[final, c, :, cols]] + [rbuf[d, :, cols] for d in range(ctxs - 1)]
-        value = functools.reduce(jnp.add, [w * x.astype(jnp.float32) for w, x in zip(weights, parts)])
-        att[final, :, cols] = (value / total).astype(jnp.bfloat16)
+        @pl.when(jnp.logical_and(g >= 2, g < merged + 2))
+        def _():
+            part_stage(g - 2, 1)
+
+        @pl.when(jnp.logical_and(g >= 3, g < merged + 3))
+        def _():
+            part_stage(g - 3, 2)
+
+        @pl.when(jnp.logical_and(g >= 4, g < merged + 4))
+        def _():
+            part_final(g - 4)
+
+    for g in range(merged):
+        if g + 2 >= groups:
+            part_stage(g, 1)
+        if g + 3 >= groups:
+            part_stage(g, 2)
+    for g in range(merged):
+        if g + 4 >= groups:
+            part_final(g)
+    for g in range(merged, groups - 1):
+        direct_final(g)
 
     @pl.loop(0, ncols)
     def _(n):
         w_copy(n).wait()
-        total = functools.reduce(jnp.add, [
+        early[n] = functools.reduce(jnp.add, [
             jnp.dot(att[g], wbuf[n, g * cw:(g + 1) * cw, :], preferred_element_type=jnp.float32)
-            for g in range(groups)])
+            for g in range(groups - 1)])
+
+    direct_final(groups - 1)
+
+    @pl.loop(0, ncols)
+    def _(n):
+        total = early[n] + jnp.dot(
+            att[groups - 1], wbuf[n, (groups - 1) * cw:, :], preferred_element_type=jnp.float32)
         pbuf[n] = total.astype(jnp.bfloat16).reshape(heads, rows, nw)
         for i in range(2):
             to_sibling(n, i).start()
@@ -432,29 +453,31 @@
         for d in range(1, heads):
             a2a(g, d, h, lax.rem(h + d, heads)).wait_send()
         for k in range(last):
-            @pl.when(jnp.logical_and(g > 0, jnp.logical_and(c < last, c >= k)))
+            @pl.when(jnp.logical_and(g >= AHEAD, jnp.logical_and(c < last, c >= k)))
             def _():
                 up(g, k, c - k).wait_send()
 
-            @pl.when(jnp.logical_and(g > 0, jnp.logical_and(c > 0, c + k <= last)))
+            @pl.when(jnp.logical_and(g >= AHEAD, jnp.logical_and(c > 0, c + k <= last)))
             def _():
                 down(g, k, c + k).wait_send()
 
         for b in range(ctxs):
-            @pl.when(jnp.logical_and(g < groups - 1, b < c))
+            @pl.when(jnp.logical_and(g < merged, b < c))
             def _():
                 for copy in part_down(g, b):
                     copy.wait_send()
 
-            @pl.when(jnp.logical_and(g < groups - 1, b > c))
+            @pl.when(jnp.logical_and(g < merged, b > c))
             def _():
                 for copy in part_up(g, b):
                     copy.wait_send()
 
     for d in range(1, ctxs):
-        gather(d, c, lax.rem(c + d, ctxs)).wait_send()
-        for copy in scatter(d, lax.rem(c + d, ctxs)):
-            copy.wait_send()
+        for g in range(AHEAD):
+            gather(g, d, c, lax.rem(c + d, ctxs)).wait_send()
+        for g in range(merged, groups):
+            for copy in scatter(g, d, lax.rem(c + d, ctxs)):
+                copy.wait_send()
 
     @pl.loop(0, ncols)
     def _(n):
@@ -487,8 +510,8 @@
             pltpu.VMEM((groups, ctxs, block, cw), bf),
             pltpu.VMEM((groups, ctxs, block, cw), bf),
             pltpu.VMEM((groups, ctxs, 8, block), f32),
-            pltpu.VMEM((ctxs - 1, block, cw), bf),
-            pltpu.VMEM((ctxs - 1, 8, block), f32),
+            pltpu.VMEM((DIRECT, ctxs - 1, block, cw), bf),
+            pltpu.VMEM((DIRECT, ctxs - 1, 8, block), f32),
             pltpu.VMEM((groups, ctxs, block, cw), bf),
             pltpu.VMEM((groups, ctxs, 8, block), f32),
             pltpu.VMEM((groups, ctxs, block, cw), bf),
@@ -502,13 +525,14 @@
             pltpu.VMEM((2, 2 * block, key_count), f32),
             pltpu.VMEM((2, 2 * block, key_count), bf),
             pltpu.VMEM((2, 2 * block, HD), f32),
+            pltpu.VMEM((ncols, block, nw), f32),
             dma((2, groups)), dma((ncols,)), dma((groups,)),
             dma((groups, ctxs - 1)), dma((groups, ctxs - 1)),
             dma((groups, ctxs - 1)), dma((groups, ctxs - 1)),
             dma((groups, 3)), dma((groups, 3)),
-            dma((ctxs - 1,)), dma((ctxs - 1,)),
-            dma((ctxs - 1,)), dma((ctxs - 1,)),
-            dma((ctxs - 1,)), dma((ctxs - 1,)),
+            dma((AHEAD, ctxs - 1)), dma((AHEAD, ctxs - 1)),
+            dma((DIRECT, ctxs - 1)), dma((DIRECT, ctxs - 1)),
+            dma((DIRECT, ctxs - 1)), dma((DIRECT, ctxs - 1)),
             dma((2, groups, ctxs)), dma((2, groups, ctxs)),
             dma((2, groups, ctxs)), dma((2, groups, ctxs)),
             dma((ncols, 2)), dma((ncols, 2)),
@@ -529,7 +553,7 @@
 
     def shards(queries, keys, values, kept_rows, out_weight):
         rows = queries.shape[0]
-        if heads == 4 and ctxs == 4 and rows == 32 and keys.shape[1] % (2 * HD) == 0:
+        if heads == 4 and ctxs == 4 and rows == 32 and keys.shape[1] == 12 * HD:
             return fused_shards(ctxs, queries, keys, values, kept_rows, out_weight)
         return general_shards(queries, keys, values, kept_rows, out_weight)
 

time: 79.5 us -> 85.8 us (1.079)
  Pallas kernels: 77.5 us -> 83.9 us
    pallas_call x1, Pallas kernels: 77.5 us -> 83.9 us  [fused_shards(): pl.pallas_call(kernel, out_shape=jax.ShapeDtypeStruct((rows, width), bf),...]
where the time goes in v6:
time: 85.8 us; the launch traced here: 85.7 us
  Pallas kernels  83.9 us (98%)
  local copies, waits for them, and re-layouts  1.77 us (2%)
    pallas_call x1, Pallas kernels, fused_shards(): pl.pallas_call(kernel, out_shape=jax.ShapeDtypeStruct((rows, width), bf),...  83.9 us
    unnamed x1, local copies, waits for them, and re-layouts  1.77 us

profile of v6, /device:TPU:0, one launch (start us, length us, event | category | flops | bytes accessed | tf_op | source)
XLA Modules:
  0.0 85.7 jit_solution(13581066292204374236)
XLA Ops:
  0.0 83.9 %attention.1 = bf16[32,6144]{1,0:T(8,128)(2,1)} custom-call(bf16[32,6144]{1,0:T(8,128)(2,1)} %q_hbm.1, bf16[2048,1536]{1,0:T(8,128)(2,1)} %k_hbm.1, bf16[2048,1536]{1,0:T(8,128)(2,1)} %v_hbm.1, s32[16]{0:T(128)} %kept_ref.1, bf16[1536,6144]{1,0:T(8,128)(2,1)} %w_hbm.1), custom_call_target="tpu_custom_call" | custom-call | flops 8858370048 | bytes 31457280 | tf_op jit(solution)/shard_map/attention/pallas_call | solution.py:501
  83.9 1.8 %copy.7 = bf16[32,6144]{1,0:T(8,128)(2,1)} copy(bf16[32,6144]{1,0:T(8,128)(2,1)} %attention.1) | data formatting | bytes 786432

commit v7 on v6

--- a/solution.py
+++ b/solution.py
@@ -10,8 +10,8 @@
 
 HD = 128
 KC = 256
-AHEAD = 2
-DIRECT = 3
+AHEAD = 1
+DIRECT = 1
 MESH = pl.DeviceIdType.MESH
 SCALE2 = math.log2(math.e) / math.sqrt(HD)
 
@@ -310,6 +310,7 @@
         gather(0, d, c, lax.rem(c + d, ctxs)).start()
     exchanged(AHEAD)
     hop(AHEAD, 0)
+    stage(AHEAD + 1)
     for g in range(1, AHEAD):
         exchanged(g)
         for d in (2, 1, 3):
@@ -389,31 +390,29 @@
         def _():
             part_stage(g, 0)
 
+        @pl.when(jnp.logical_and(g >= 1, g < merged + 1))
+        def _():
+            part_stage(g - 1, 1)
+
+        @pl.when(jnp.logical_and(g >= 2, g < merged + 2))
+        def _():
+            part_stage(g - 2, 2)
+
         @pl.when(g >= merged)
         def _():
             for d in (2, 1, 3):
                 for copy in scatter(g, d, lax.rem(c + d, ctxs)):
                     copy.start()
 
-        @pl.when(jnp.logical_and(g >= 2, g < merged + 2))
-        def _():
-            part_stage(g - 2, 1)
-
         @pl.when(jnp.logical_and(g >= 3, g < merged + 3))
         def _():
-            part_stage(g - 3, 2)
-
-        @pl.when(jnp.logical_and(g >= 4, g < merged + 4))
-        def _():
-            part_final(g - 4)
+            part_final(g - 3)
 
     for g in range(merged):
         if g + 2 >= groups:
-            part_stage(g, 1)
-        if g + 3 >= groups:
             part_stage(g, 2)
     for g in range(merged):
-        if g + 4 >= groups:
+        if g + 3 >= groups:
             part_final(g)
     for g in range(merged, groups - 1):
         direct_final(g)

time: 85.8 us -> 80.2 us (0.935)
  Pallas kernels: 83.9 us -> 78.2 us
    pallas_call x1, Pallas kernels: 83.9 us -> 78.2 us  [fused_shards(): pl.pallas_call(kernel, out_shape=jax.ShapeDtypeStruct((rows, width), bf),...]
where the time goes in v7:
time: 80.2 us; the launch traced here: 80 us
  Pallas kernels  78.2 us (98%)
  local copies, waits for them, and re-layouts  1.77 us (2%)
    pallas_call x1, Pallas kernels, fused_shards(): pl.pallas_call(kernel, out_shape=jax.ShapeDtypeStruct((rows, width), bf),...  78.2 us
    unnamed x1, local copies, waits for them, and re-layouts  1.77 us

profile of v7, /device:TPU:0, one launch (start us, length us, event | category | flops | bytes accessed | tf_op | source)
XLA Modules:
  0.0 80.0 jit_solution(2954558488816139466)
XLA Ops:
  0.0 78.2 %attention.1 = bf16[32,6144]{1,0:T(8,128)(2,1)} custom-call(bf16[32,6144]{1,0:T(8,128)(2,1)} %q_hbm.1, bf16[2048,1536]{1,0:T(8,128)(2,1)} %k_hbm.1, bf16[2048,1536]{1,0:T(8,128)(2,1)} %v_hbm.1, s32[16]{0:T(128)} %kept_ref.1, bf16[1536,6144]{1,0:T(8,128)(2,1)} %w_hbm.1), custom_call_target="tpu_custom_call" | custom-call | flops 8858370048 | bytes 31457280 | tf_op jit(solution)/shard_map/attention/pallas_call | solution.py:500
  78.2 1.8 %copy.7 = bf16[32,6144]{1,0:T(8,128)(2,1)} copy(bf16[32,6144]{1,0:T(8,128)(2,1)} %attention.1) | data formatting | bytes 786432
